TPU v7x, 32 devices: a whole 2x2x4 slice. The times are simulated.
32 devices in a mesh: rep: 16 (over z, y, core), shard: 2 (over x).
Axes of the slice: x: 2, y: 2, z: 4, core: 2. Of those that a mesh axis runs over, the one named last changes fastest.
Arguments:
- hidden_in: bfloat16 [32768, 1536], P(('rep', 'shard')), may hold values from -6 to 6
- segment_ids: int32 [32, 1024], P(('rep', 'shard')), may hold values from 0 to 3, never falling along the last dimension, each value on 1 to 512 neighbouring positions
- norm_gain: float32 [1536], P('shard'), may hold values from 0.25 to 1.75
- in_weight: bfloat16 [1536, 6448], P('shard'), may hold values from -0.15625 to 0.15625
- conv_weight: float32 [4, 3328], P(None, 'shard'), may hold values from -3 to 3
- conv_bias: float32 [3328], P('shard'), may hold values from -3 to 3
- dt_bias: float32 [48], P('shard'), may hold values from -5 to -1.5
- a_log: float32 [48], P('shard'), may hold values from 0 to 2.77
- d_skip: float32 [48], P('shard'), may hold values from 0.3 to 1.7
- gate_gain: float32 [3072], P('shard'), may hold values from 0.25 to 1.75
- out_weight: bfloat16 [3072, 1536], P('shard'), may hold values from -0.109375 to 0.109375
- cotangent: bfloat16 [32768, 1536], P(('rep', 'shard')), may hold values from -6 to 6
Outputs:
- block_out: bfloat16 [32768, 1536], P(('rep', 'shard'))
- input_grad: float32 [32768, 1536], P(('rep', 'shard'))
- grad_norm_gain: float32 [1536], P('shard')
- grad_in_weight: float32 [1536, 6448], P('shard')
- grad_conv_weight: float32 [4, 3328], P(None, 'shard')
- grad_conv_bias: float32 [3328], P('shard')
- grad_dt_bias: float32 [48], P('shard')
- grad_a_log: float32 [48], P('shard')
- grad_d_skip: float32 [48], P('shard')
- grad_gate_gain: float32 [3072], P('shard')
- grad_out_weight: float32 [3072, 1536], P('shard')
Inputs may be any that keep to these rules, and one draw needn't show every extreme that they name: `segment_ids`: in each packed row the numbers never fall, each of 0 to 3 occurs in one run of 1 to 512 tokens, and one run has exactly 512.
All inputs are finite; a program needn't handle non-finite values.
Results may differ from a plain program's by a relative error of at most 0.0075.
Values may be sent and summed in bfloat16 or wider, within the bound.
A program may use at most 384 MiB of HBM per device.

v0:
```python
import jax
import jax.numpy as jnp
from jax import lax
from jax.sharding import PartitionSpec as P

H = 48
HEADDIM = 64
N = 128
CONV = 4
SPAN = 256


EPS = 1e-05
HIGH = lax.Precision.HIGHEST


def conv_row(channels, segments, conv_weight, conv_bias):
    length = channels.shape[0]
    padded = jnp.concatenate(
        [jnp.zeros((CONV - 1, channels.shape[1]), jnp.float32), channels], axis=0
    )
    seg_padded = jnp.concatenate([jnp.full((CONV - 1,), -1, jnp.int32), segments], axis=0)
    summed = conv_bias[None, :] + jnp.zeros_like(channels)
    for offset in range(CONV):
        same_seg = (seg_padded[offset : offset + length] == segments).astype(jnp.float32)
        summed = (
            summed
            + conv_weight[offset][None, :] * padded[offset : offset + length] * same_seg[:, None]
        )
    return summed


def span_step(carry, block):
    state, seg_prev = carry
    signal, steps_dt, log_decay, inputs_b, readout, segments = block
    cumulated = jnp.cumsum(log_decay, axis=0)
    count = segments.shape[0]
    position = jnp.arange(count)
    causal = (position[:, None] >= position[None, :]) & (segments[:, None] == segments[None, :])
    spread_log = cumulated.T[:, :, None] - cumulated.T[:, None, :]
    decayed = jnp.exp(jnp.where(causal[None], spread_log, -1e30))
    scores = jnp.dot(readout, inputs_b.T, precision=HIGH)
    scaled_x = signal * steps_dt[:, :, None]
    within = jnp.einsum("hts,shp->thp", decayed * scores[None], scaled_x, precision=HIGH)
    carried = (segments == seg_prev).astype(jnp.float32)
    from_state = (
        jnp.einsum("tn,hpn->thp", readout, state, precision=HIGH)
        * (jnp.exp(cumulated) * carried[:, None])[:, :, None]
    )
    last_seg = segments[count - 1]
    to_end = (
        jnp.exp(cumulated[count - 1][None, :] - cumulated)
        * (segments == last_seg).astype(jnp.float32)[:, None]
    )
    kept_share = jnp.exp(cumulated[count - 1]) * (last_seg == seg_prev).astype(jnp.float32)
    new_state = state * kept_share[:, None, None] + jnp.einsum(
        "sh,shp,sn->hpn", to_end, scaled_x, inputs_b, precision=HIGH
    )
    return ((new_state, last_seg), within + from_state)


def scan_row(signal, steps_dt, log_decay, inputs_b, readout, segments):
    blocks = signal.shape[0] // SPAN

    def split(value):
        return value.reshape((blocks, SPAN) + value.shape[1:])

    start_state = jnp.zeros((H, HEADDIM, N), jnp.float32)
    _, outputs = lax.scan(
        jax.checkpoint(span_step),
        (start_state, segments[0]),
        (
            split(signal),
            split(steps_dt),
            split(log_decay),
            split(inputs_b),
            split(readout),
            split(segments),
        ),
    )
    return outputs.reshape(signal.shape)


def mixer_row(
    gate_z, channels, dt_raw, segments, conv_weight, conv_bias, dt_bias, a_log, d_skip, gate_gain
):
    length = gate_z.shape[0]
    inner = H * HEADDIM
    activated = jax.nn.silu(conv_row(channels, segments, conv_weight, conv_bias))
    signal = activated[:, :inner].reshape(length, H, HEADDIM)
    inputs_b = activated[:, inner : inner + N]
    readout = activated[:, inner + N :]
    steps_dt = jax.nn.softplus(dt_raw + dt_bias[None, :])
    log_decay = -jnp.exp(a_log)[None, :] * steps_dt
    outputs = (
        scan_row(signal, steps_dt, log_decay, inputs_b, readout, segments)
        + d_skip[None, :, None] * signal
    )
    gated = outputs.reshape(length, inner) * jax.nn.silu(gate_z)
    factor = lax.rsqrt(jnp.mean(gated * gated, axis=1, keepdims=True) + EPS)
    return gated * factor * gate_gain[None, :]


def mixer_rows(mixed, segment_ids, conv_weight, conv_bias, dt_bias, a_log, d_skip, gate_gain):
    rows, length = segment_ids.shape
    inner = H * HEADDIM
    width = conv_weight.shape[1]
    grouped = mixed.reshape(rows, length, mixed.shape[1])

    def one_row(block, segments):
        return mixer_row(
            block[:, :inner],
            block[:, inner : inner + width],
            block[:, inner + width :],
            segments,
            conv_weight,
            conv_bias,
            dt_bias,
            a_log,
            d_skip,
            gate_gain,
        )

    return jax.vmap(one_row)(grouped, segment_ids).reshape(rows * length, inner)


def prenorm(hidden, gain):
    factor = lax.rsqrt(jnp.mean(hidden * hidden, axis=1, keepdims=True) + EPS)
    return hidden * factor * gain[None, :]


def contract_rows(left, right):
    return lax.dot_general(
        left, right, (((0,), (0,)), ((), ())), preferred_element_type=jnp.float32
    )


def contract_cols(left, right):
    return lax.dot_general(
        left, right, (((1,), (1,)), ((), ())), preferred_element_type=jnp.float32
    )


def body(
    hidden_in,
    segment_ids,
    norm_gain,
    in_weight,
    conv_weight,
    conv_bias,
    dt_bias,
    a_log,
    d_skip,
    gate_gain,
    out_weight,
    cotangent,
):
    full_gain, full_cbias, full_dtbias, full_alog, full_skip, full_ggain, full_cweight = (
        lax.all_gather(norm_gain, "shard", axis=0, tiled=True),
        lax.all_gather(conv_bias, "shard", axis=0, tiled=True),
        lax.all_gather(dt_bias, "shard", axis=0, tiled=True),
        lax.all_gather(a_log, "shard", axis=0, tiled=True),
        lax.all_gather(d_skip, "shard", axis=0, tiled=True),
        lax.all_gather(gate_gain, "shard", axis=0, tiled=True),
        lax.all_gather(conv_weight, "shard", axis=1, tiled=True),
    )
    hidden = hidden_in.astype(jnp.float32)
    normed, pre_back = jax.vjp(prenorm, hidden, full_gain)
    normed_low = normed.astype(jnp.bfloat16)
    whole_in, whole_out = (
        lax.all_gather(in_weight, "shard", axis=0, tiled=True),
        lax.all_gather(out_weight, "shard", axis=0, tiled=True),
    )
    mixed = jnp.dot(normed_low, whole_in, preferred_element_type=jnp.float32)

    def mixer_local(mixed, cweight, cbias, dtbias, alog, skip, ggain):
        return mixer_rows(mixed, segment_ids, cweight, cbias, dtbias, alog, skip, ggain)

    gnormed, mix_back = jax.vjp(
        mixer_local, mixed, full_cweight, full_cbias, full_dtbias, full_alog, full_skip, full_ggain
    )
    gnormed_low = gnormed.astype(jnp.bfloat16)
    branch_out = jnp.dot(gnormed_low, whole_out, preferred_element_type=jnp.float32)
    block_out = (hidden + branch_out).astype(jnp.bfloat16)
    grad_outer = contract_rows(gnormed_low, cotangent)
    d_gnormed = contract_cols(cotangent, whole_out)
    d_mixed, grad_cweight, grad_cbias, grad_dtbias, grad_alog, grad_skip, grad_ggain = mix_back(
        d_gnormed
    )
    d_mixed_low = d_mixed.astype(jnp.bfloat16)
    grad_inner = contract_rows(normed_low, d_mixed_low)
    d_normed = contract_cols(d_mixed_low, whole_in)
    d_hidden, grad_gain = pre_back(d_normed)
    input_grad = cotangent.astype(jnp.float32) + d_hidden
    owned = (
        lax.psum_scatter(grad_gain, "shard", scatter_dimension=0, tiled=True),
        lax.psum_scatter(grad_inner, "shard", scatter_dimension=0, tiled=True),
        lax.psum_scatter(grad_cweight, "shard", scatter_dimension=1, tiled=True),
        lax.psum_scatter(grad_cbias, "shard", scatter_dimension=0, tiled=True),
        lax.psum_scatter(grad_dtbias, "shard", scatter_dimension=0, tiled=True),
        lax.psum_scatter(grad_alog, "shard", scatter_dimension=0, tiled=True),
        lax.psum_scatter(grad_skip, "shard", scatter_dimension=0, tiled=True),
        lax.psum_scatter(grad_ggain, "shard", scatter_dimension=0, tiled=True),
        lax.psum_scatter(grad_outer, "shard", scatter_dimension=0, tiled=True),
    )
    owned = lax.psum(
        (owned[0], owned[1], owned[2], owned[3], owned[4], owned[5], owned[6], owned[7], owned[8]),
        "rep",
    )
    (
        own_gain,
        own_inner,
        own_cweight,
        own_cbias,
        own_dtbias,
        own_alog,
        own_skip,
        own_ggain,
        own_outer,
    ) = owned
    return (
        block_out,
        input_grad,
        own_gain,
        own_inner,
        own_cweight,
        own_cbias,
        own_dtbias,
        own_alog,
        own_skip,
        own_ggain,
        own_outer,
    )


def solution(mesh):
    in_specs = (
        P(("rep", "shard"), None),
        P(("rep", "shard"), None),
        P("shard"),
        P("shard", None),
        P(None, "shard"),
        P("shard"),
        P("shard"),
        P("shard"),
        P("shard"),
        P("shard"),
        P("shard", None),
        P(("rep", "shard"), None),
    )
    out_specs = (
        P(("rep", "shard"), None),
        P(("rep", "shard"), None),
        P("shard"),
        P("shard", None),
        P(None, "shard"),
        P("shard"),
        P("shard"),
        P("shard"),
        P("shard"),
        P("shard"),
        P("shard", None),
    )
    return jax.shard_map(body, mesh=mesh, in_specs=in_specs, out_specs=out_specs, check_vma=False)
```

profile of v0, /device:TPU:0, one launch (start us, length us, event | category | flops | bytes accessed | tf_op | source)
XLA Modules:
  0.0 2887.4 jit_solution(1125606797655524469)
XLA Ops:
  41.0 206.6 %all-gather.6.cloned.1.call-done = bf16[1536,6448]{0,1:T(8,128)(2,1)} async-done(((bf16[768,6448]{0,1:T(8,128)(2,1)}), bf16[1536,6448]{0,1:T(8,128)(2,1)}) %all-gather.6.cloned.1.call-update) | async-done | bytes 19808272 | tf_op jit(solution)/shard_map/all_gather | solution.py:171
  247.6 28.2 convolution_bitcast_fusion.1
  288.7 33.1 %fusion.114 = (f32[1,1024,3328]{1,2,0:T(8,128)}, f32[1,1024,3328]{1,2,0:T(8,128)}) fusion(f32[1,1024,3328]{1,2,0:T(8,128)} %slice.162, f32[3328]{0:T(1024)S(1)} %get-tuple-element.769, f32[1024]{0:T(1024)S(1)} %bitcast.619, f32[3328]{0:T(1024)S(1)} %get-tuple-element.770, f32[1024]{0:T(1024)S(1)} %bitcast.622, f32[3328]{0:T(1024)S(1)} %get-tuple-element.771, ...), kind=kLoop, calls=%fused_computation.176 | loop fusion | flops 51118080 | bytes 40973312 | tf_op jit(solution)/shard_map/jvp(vmap(jit(silu)))/mul | solution.py:89
  339.7 15.8 reshape.1255
  375.0 431.6 %while.45 = (s32[]{:T(128)}, f32[1,48,64,128]{3,2,1,0:T(8,128)S(1)}, s32[1]{0:T(128)}, f32[4,1,256,48,64]{2,0,4,3,1:T(4,128)}, f32[4,1,48,64,128]{4,3,2,1,0:T(8,...) while((s32[]{:T(128)}, ...), condition=%wide.region_4.5_spmd.clone, body=%wide.region_1.4_spmd.clone.sunk | while | flops 4949656576 | bytes 38946236 | solution.py:69
  414.6 68.2 %dynamic_update_slice.84 = f32[4,1,256,48,64]{2,0,4,3,1:T(4,128)} dynamic-update-slice(f32[4,1,256,48,64]{2,0,4,3,1:T(4,128)} %get-tuple-element.1146, f32[1,1,256,48,64]{2,0,4,3,1:T(1,128)} %copy.352, s32[]{:T(128)S(6)} %copy.389, s32[]{:T(128)} %constant.136.clone.1..sunk, s32[]{:T(128)} %constant.136.clone.1..sunk, s32[]{:T(128)} %constant.136.clone.1..sunk, s32[]{:T(128)} %constant.136.clone.1..sunk) | dynamic-update-slice | bytes 6291460 | tf_op jit(solution)/shard_map/jvp(vmap())/while/body/jit(dynamic_update_index_in_dim)/dynamic_update_slice | solution.py:69
  522.5 68.2 %dynamic_update_slice.84 = f32[4,1,256,48,64]{2,0,4,3,1:T(4,128)} dynamic-update-slice(f32[4,1,256,48,64]{2,0,4,3,1:T(4,128)} %get-tuple-element.1146, f32[1,1,256,48,64]{2,0,4,3,1:T(1,128)} %copy.352, s32[]{:T(128)S(6)} %copy.389, s32[]{:T(128)} %constant.136.clone.1..sunk, s32[]{:T(128)} %constant.136.clone.1..sunk, s32[]{:T(128)} %constant.136.clone.1..sunk, s32[]{:T(128)} %constant.136.clone.1..sunk) | dynamic-update-slice | bytes 6291460 | tf_op jit(solution)/shard_map/jvp(vmap())/while/body/jit(dynamic_update_index_in_dim)/dynamic_update_slice | solution.py:69
  630.4 68.2 %dynamic_update_slice.84 = f32[4,1,256,48,64]{2,0,4,3,1:T(4,128)} dynamic-update-slice(f32[4,1,256,48,64]{2,0,4,3,1:T(4,128)} %get-tuple-element.1146, f32[1,1,256,48,64]{2,0,4,3,1:T(1,128)} %copy.352, s32[]{:T(128)S(6)} %copy.389, s32[]{:T(128)} %constant.136.clone.1..sunk, s32[]{:T(128)} %constant.136.clone.1..sunk, s32[]{:T(128)} %constant.136.clone.1..sunk, s32[]{:T(128)} %constant.136.clone.1..sunk) | dynamic-update-slice | bytes 6291460 | tf_op jit(solution)/shard_map/jvp(vmap())/while/body/jit(dynamic_update_index_in_dim)/dynamic_update_slice | solution.py:69
  738.3 68.2 %dynamic_update_slice.84 = f32[4,1,256,48,64]{2,0,4,3,1:T(4,128)} dynamic-update-slice(f32[4,1,256,48,64]{2,0,4,3,1:T(4,128)} %get-tuple-element.1146, f32[1,1,256,48,64]{2,0,4,3,1:T(1,128)} %copy.352, s32[]{:T(128)S(6)} %copy.389, s32[]{:T(128)} %constant.136.clone.1..sunk, s32[]{:T(128)} %constant.136.clone.1..sunk, s32[]{:T(128)} %constant.136.clone.1..sunk, s32[]{:T(128)} %constant.136.clone.1..sunk) | dynamic-update-slice | bytes 6291460 | tf_op jit(solution)/shard_map/jvp(vmap())/while/body/jit(dynamic_update_index_in_dim)/dynamic_update_slice | solution.py:69
  806.6 15.7 transpose.180
  853.7 20.5 fusion.118
  874.3 33.3 %multiply_reduce_fusion.7 = (f32[3072]{0:T(1024)}, f32[1,1024,3072]{1,2,0:T(8,128)}, f32[1,1024,3072]{1,2,0:T(8,128)}) fusion(f32[1,1024,3328]{1,2,0:T(8,128)} %get-tuple-element.857, f32[1,1024,6448]{1,2,0:T(8,128)} %convolution_bitcast_fusion.1, f32[1,1024,3072]{1,2,0:T(8,128)} %copy-done.2, f32[1024]{0:T(1024)S(1)} %multiply_multiply_fusion.4, ...), kind=kLoop, calls=%fused_computation.188 | loop fusion | flops 66057216 | bytes 88125440 | tf_op jit(solution)/shard_map/transpose(jvp(vmap()))/reduce_sum | solution.py:97
  907.6 15.5 reshape.1259
  933.7 812.4 %while.46 = (s32[]{:T(128)}, f32[1,48,64,128]{3,2,1,0:T(8,128)}, f32[4,1,256,48,64]{2,0,4,3,1:T(4,128)}, f32[4,1,256,48]{2,0,3,1:T(4,128)}, f32[4,1,256,48]{2,0,...) while((s32[]{:T(128)}, f32[1,48,64,128]{3,2,1,0:T(8,128)}, ...), condition=%wide.region_19.20_spmd.clone, body=%wide.region_7.19_spmd.clone.sunk | while | flops 11228652544 | bytes 116231752 | solution.py:69
  1009.2 19.9 fusion.233
  1084.4 67.9 %dynamic_update_slice.87 = f32[4,1,256,48,64]{2,0,4,3,1:T(4,128)} dynamic-update-slice(f32[4,1,256,48,64]{2,0,4,3,1:T(4,128)} %get-tuple-element.1195, f32[1,1,256,48,64]{2,0,4,3,1:T(1,128)S(1)} %copy.366, s32[]{:T(128)S(6)} %sub.218, s32[]{:T(128)} %constant.136.clone.1..sunk.1, s32[]{:T(128)} %constant.136.clone.1..sunk.1, s32[]{:T(128)} %constant.136.clone.1..sunk.1, s32[]{:T(128)} %constant.136.clone.1..sunk.1) | dynamic-update-slice | bytes 6291460 | tf_op jit(solution)/shard_map/transpose(jvp(vmap()))/while/body/jit(dynamic_update_index_in_dim)/dynamic_update_slice | solution.py:69
  1205.6 19.9 fusion.233
  1280.4 67.9 %dynamic_update_slice.87 = f32[4,1,256,48,64]{2,0,4,3,1:T(4,128)} dynamic-update-slice(f32[4,1,256,48,64]{2,0,4,3,1:T(4,128)} %get-tuple-element.1195, f32[1,1,256,48,64]{2,0,4,3,1:T(1,128)S(1)} %copy.366, s32[]{:T(128)S(6)} %sub.218, s32[]{:T(128)} %constant.136.clone.1..sunk.1, s32[]{:T(128)} %constant.136.clone.1..sunk.1, s32[]{:T(128)} %constant.136.clone.1..sunk.1, s32[]{:T(128)} %constant.136.clone.1..sunk.1) | dynamic-update-slice | bytes 6291460 | tf_op jit(solution)/shard_map/transpose(jvp(vmap()))/while/body/jit(dynamic_update_index_in_dim)/dynamic_update_slice | solution.py:69
  1401.6 19.9 fusion.233
  1476.5 67.9 %dynamic_update_slice.87 = f32[4,1,256,48,64]{2,0,4,3,1:T(4,128)} dynamic-update-slice(f32[4,1,256,48,64]{2,0,4,3,1:T(4,128)} %get-tuple-element.1195, f32[1,1,256,48,64]{2,0,4,3,1:T(1,128)S(1)} %copy.366, s32[]{:T(128)S(6)} %sub.218, s32[]{:T(128)} %constant.136.clone.1..sunk.1, s32[]{:T(128)} %constant.136.clone.1..sunk.1, s32[]{:T(128)} %constant.136.clone.1..sunk.1, s32[]{:T(128)} %constant.136.clone.1..sunk.1) | dynamic-update-slice | bytes 6291460 | tf_op jit(solution)/shard_map/transpose(jvp(vmap()))/while/body/jit(dynamic_update_index_in_dim)/dynamic_update_slice | solution.py:69
  1597.7 19.9 fusion.233
  1672.5 67.9 %dynamic_update_slice.87 = f32[4,1,256,48,64]{2,0,4,3,1:T(4,128)} dynamic-update-slice(f32[4,1,256,48,64]{2,0,4,3,1:T(4,128)} %get-tuple-element.1195, f32[1,1,256,48,64]{2,0,4,3,1:T(1,128)S(1)} %copy.366, s32[]{:T(128)S(6)} %sub.218, s32[]{:T(128)} %constant.136.clone.1..sunk.1, s32[]{:T(128)} %constant.136.clone.1..sunk.1, s32[]{:T(128)} %constant.136.clone.1..sunk.1, s32[]{:T(128)} %constant.136.clone.1..sunk.1) | dynamic-update-slice | bytes 6291460 | tf_op jit(solution)/shard_map/transpose(jvp(vmap()))/while/body/jit(dynamic_update_index_in_dim)/dynamic_update_slice | solution.py:69
  1750.8 15.8 transpose.185
  1782.3 33.0 %multiply_reduce_fusion.5 = (f32[3328]{0:T(1024)S(1)}, f32[3328]{0:T(1024)S(1)}, f32[3328]{0:T(1024)S(1)}, f32[3328]{0:T(1024)S(1)}, f32[3328]{0:T(1024)S(1)}, /*index=5*/f32[1,1024,3328]{1,2,0:T(8,128)}) fusion(f32[1,1024,3328]{1,2,0:T(8,128)} %slice.162, f32[1024]{0:T(1024)S(1)} %bitcast.620, f32[1024]{0:T(1024)S(1)} %bitcast.623, f32[1024]{0:T(1024)S(1)} %bitcast.617, ...), kind=kLoop, calls=%fused_computation.173 | loop fusion | flops 78364416 | bytes 68236288 | tf_op jit(solution)/shard_map/transpose(jvp(vmap()))/reduce_sum | solution.py:28
  1815.3 18.0 broadcast_multiply_fusion
  1833.4 20.8 pad_add_fusion
  1854.1 33.5 %fusion.132 = f32[1536,6448]{0,1:T(8,128)} fusion(bf16[1024,1536]{1,0:T(8,128)(2,1)S(1)} %copy-done.3, f32[1536]{0:T(1024)S(1)} %copy-done.32, f32[1024]{0:T(1024)S(1)} %copy-done.37, f32[1,1024,3072]{1,2,0:T(8,128)} %get-tuple-element.877, f32[1,1024,3328]{1,2,0:T(8,128)} %pad_add_fusion, f32[1,1024,48]{1,2,0:T(8,128)S(1)} %get-tuple-element.853), kind=kOutput, calls=%fused_computation.213 | convolution fusion | flops 20309753856 | bytes 69183488 | tf_op jit(solution)/shard_map/dot_general | solution.py:133
  1889.7 432.4 %reduce-scatter.6.cloned.1.call-done = f32[768,6448]{0,1:T(8,128)} async-done(((f32[1536,6448]{0,1:T(8,128)}), f32[768,6448]{0,1:T(8,128)}) %reduce-scatter.6.cloned.1.call-update) | async-done | bytes 19808272 | tf_op jit(solution)/shard_map/reduce_scatter | solution.py:197
  2324.5 33.0 %fusion.124 = (f32[1536]{0:T(1024)S(1)}, f32[1024]{0:T(1024)S(1)}, f32[1024,1536]{1,0:T(8,128)}) fusion(bf16[1024,1536]{1,0:T(8,128)(2,1)S(1)} %copy-done.3, f32[1024]{0:T(1024)S(1)} %copy-done.37, f32[1536]{0:T(1024)S(1)} %copy-done.32, bf16[1536,6448]{0,1:T(8,128)(2,1)} %all-gather.6.cloned.1.call-done, f32[1,1024,3072]{1,2,0:T(8,128)} %get-tuple-element.877, ...), kind=kOutput, calls=%fused_computation.205 | convolution fusion | flops 20314468352 | bytes 55676928 | tf_op jit(solution)/shard_map/dot_general | solution.py:139
  2372.0 17.4 fusion.127
  2390.9 63.9 %all-reduce.27 = (f32[768]{0:T(1024)}, f32[4,1664]{1,0:T(4,128)}, f32[1664]{0:T(1024)}, f32[24]{0:T(128)}, f32[24]{0:T(128)}, /*index=5*/f32[24]{0:T(128)}, f32[1536]{0:T(1024)}) all-reduce(f32[768]{0:T(1024)S(1)} %dynamic-slice.4, f32[4,1664]{1,0:T(4,128)S(1)} %copy.258, ...), channel_id=1, replica_groups=mesh['rep'=16,'shard'=2] {'rep'}, use_global_device_ids=true, to_apply=%region_23.24 | all-reduce | flops 10696 | bytes 85568 | tf_op jit(solution)/shard_map/psum | solution.py:206
  2454.8 405.3 %all-reduce.33.cloned.1.call-done = (f32[768,6448]{0,1:T(8,128)}, f32[1536,1536]{1,0:T(8,128)}) async-done(((f32[768,6448]{0,1:T(8,128)}, f32[1536,1536]{1,0:T(8,128)}), (f32[768,6448]{0,1:T(8,128)}, f32[1536,1536]{1,0:T(8,128)})) %all-reduce.33.cloned.1.call-update) | async-done | bytes 29245456 | tf_op jit(solution)/shard_map/psum | solution.py:206
  (572 shorter events, 763.1 us)
Async XLA Ops:
  7.3 23.2 copy-start.40
  7.3 28.4 copy-start.33
  7.3 240.4 %all-gather.6.cloned.1.call-start = ((), (), s32[]{:S(2)}) async-start(), calls=%async_computation.3 | async-start | bytes 29712384 | tf_op jit(solution)/shard_map/all_gather | solution.py:171
  8.0 845.7 %all-gather.8.cloned.1.call-start = ((), (), s32[]{:S(2)}) async-start(), calls=%async_computation.4 | async-start | bytes 14155776 | tf_op jit(solution)/shard_map/all_gather | solution.py:172
  8.8 1880.9 %reduce-scatter.8.cloned.1.call-start = ((), (), s32[]{:S(2)}) async-start(), calls=%async_computation.6 | async-start | bytes 28311552 | tf_op jit(solution)/shard_map/reduce_scatter | solution.py:204
  9.5 279.2 %copy-start.20 = (f32[1,1024]{1,0:T(1,128)}, f32[1,1024]{1,0:T(1,128)S(1)}, u32[]{:S(2)}) copy-start(f32[1,1024]{1,0:T(1,128)S(1)} %get-tuple-element.885) | copy-start | bytes 12292
  9.5 279.2 %copy-start.22 = (f32[1,1024]{1,0:T(1,128)}, f32[1,1024]{1,0:T(1,128)S(1)}, u32[]{:S(2)}) copy-start(f32[1,1024]{1,0:T(1,128)S(1)} %get-tuple-element.886) | copy-start | bytes 12292
  9.5 279.2 %copy-start.24 = (f32[1,1024]{1,0:T(1,128)}, f32[1,1024]{1,0:T(1,128)S(1)}, u32[]{:S(2)}) copy-start(f32[1,1024]{1,0:T(1,128)S(1)} %get-tuple-element.887) | copy-start | bytes 12292
  17.3 317.8 %copy-start.42 = (f32[48]{0:T(128)}, f32[48]{0:T(128)S(1)}, u32[]{:S(2)}) copy-start(f32[48]{0:T(128)S(1)} %get-tuple-element.843) | copy-start | bytes 580
  17.9 317.2 %copy-start.44 = (f32[48]{0:T(128)}, f32[48]{0:T(128)S(1)}, u32[]{:S(2)}) copy-start(f32[48]{0:T(128)S(1)} %exponential_negate_fusion) | copy-start | bytes 580
  22.3 253.6 %copy-start.31 = (f32[1536]{0:T(1024)}, f32[1536]{0:T(1024)S(1)}, u32[]{:S(2)}) copy-start(f32[1536]{0:T(1024)S(1)} %reshape.1278) | copy-start | bytes 18436
  26.0 249.9 %copy-start.36 = (f32[1024]{0:T(1024)}, f32[1024]{0:T(1024)S(1)}, u32[]{:S(2)}) copy-start(f32[1024]{0:T(1024)S(1)} %fusion.138) | copy-start | bytes 12292
  41.0 247.7 %copy-start.11 = (f32[3328]{0:T(1024)}, f32[3328]{0:T(1024)S(1)}, u32[]{:S(2)}) copy-start(f32[3328]{0:T(1024)S(1)} %get-tuple-element.768) | copy-start | bytes 39940
  41.0 247.7 %copy-start.13 = (f32[3328]{0:T(1024)}, f32[3328]{0:T(1024)S(1)}, u32[]{:S(2)}) copy-start(f32[3328]{0:T(1024)S(1)} %get-tuple-element.769) | copy-start | bytes 39940
  41.0 247.7 %copy-start.15 = (f32[3328]{0:T(1024)}, f32[3328]{0:T(1024)S(1)}, u32[]{:S(2)}) copy-start(f32[3328]{0:T(1024)S(1)} %get-tuple-element.770) | copy-start | bytes 39940
  41.0 247.7 %copy-start.17 = (f32[3328]{0:T(1024)}, f32[3328]{0:T(1024)S(1)}, u32[]{:S(2)}) copy-start(f32[3328]{0:T(1024)S(1)} %get-tuple-element.771) | copy-start | bytes 39940
  836.0 38.3 %copy-start.34 = (f32[1024]{0:T(1024)}, f32[1024]{0:T(1024)S(1)}, u32[]{:S(2)}) copy-start(f32[1024]{0:T(1024)S(1)} %fusion.139) | copy-start | bytes 12292
  874.3 1447.8 %reduce-scatter.6.cloned.1.call-start = ((), (), s32[]{:S(2)}) async-start(), calls=%async_computation.5 | async-start | bytes 59424768 | tf_op jit(solution)/shard_map/reduce_scatter | solution.py:197
  1401.6 19.9 copy-start.5
  1597.7 19.9 copy-start.5
  1782.2 33.0 %copy-start.12 = (f32[3328]{0:T(1024)S(1)}, f32[3328]{0:T(1024)}, u32[]{:S(2)}) copy-start(f32[3328]{0:T(1024)} %copy-done.11) | copy-start | bytes 39940
  1782.3 33.0 %copy-start.14 = (f32[3328]{0:T(1024)S(1)}, f32[3328]{0:T(1024)}, u32[]{:S(2)}) copy-start(f32[3328]{0:T(1024)} %copy-done.13) | copy-start | bytes 39940
  1782.3 33.0 %copy-start.16 = (f32[3328]{0:T(1024)S(1)}, f32[3328]{0:T(1024)}, u32[]{:S(2)}) copy-start(f32[3328]{0:T(1024)} %copy-done.15) | copy-start | bytes 39940
  1782.3 33.0 %copy-start.18 = (f32[3328]{0:T(1024)S(1)}, f32[3328]{0:T(1024)}, u32[]{:S(2)}) copy-start(f32[3328]{0:T(1024)} %copy-done.17) | copy-start | bytes 39940
  1833.4 20.8 copy-start.3
  1833.4 20.8 copy-start.32
  1833.4 20.8 copy-start.37
  1887.6 501.8 %reduce-scatter.10.cloned.1.call-start = ((), (), s32[]{:S(2)}) async-start(), calls=%async_computation.7 | async-start | bytes 2555904
  1889.6 970.4 %all-reduce.33.cloned.1.call-start = ((), (), s32[]{:S(2)}) async-start(), calls=%async_computation.8 | async-start | bytes 58490880 | tf_op jit(solution)/shard_map/psum | solution.py:206
  2324.5 33.0 %copy-start.38 = (f32[3072]{0:T(1024)S(1)}, f32[3072]{0:T(1024)}, u32[]{:S(2)}) copy-start(f32[3072]{0:T(1024)} %get-tuple-element.762) | copy-start | bytes 36868
  2324.5 33.0 %copy-start.46 = (f32[48]{0:T(128)S(1)}, f32[48]{0:T(128)}, u32[]{:S(2)}) copy-start(f32[48]{0:T(128)} %get-tuple-element.852) | copy-start | bytes 580
  2324.5 40.8 %copy-start.30 = (f32[1024]{0:T(1024)S(1)}, f32[1024]{0:T(1024)}, u32[]{:S(2)}) copy-start(f32[1024]{0:T(1024)} %copy-done.29) | copy-start | bytes 12292
  (36 other events, 424.8 us)
Sparse Core Ops, SparseCore 0:
  9.7 237.9 all-gather.5
  249.2 117.9 all-gather.7
  874.4 211.7 reduce-scatter.7
  1887.8 434.2 reduce-scatter.5
  2324.7 27.5 reduce-scatter.9
  2357.1 502.8 all-reduce.32
where the time goes:
time: 2910 us; the launch traced here: 2890 us
  waiting for transfers between devices  1050 us (36%)
  local copies, waits for them, and re-layouts  921 us (32%)
  matrix products  506 us (17%)
  other arithmetic  260 us (9%)
  blocking collectives  95.4 us (3%)
  loops' own time  40.9 us (1%)
    dynamic_update_slice x40, local copies, waits for them, and re-layouts, scan_row(): lax.scan(jax.checkpoint(span_step), (start_state, segments[0]), (split(si...  616 us
    reduce_scatter x1, waiting for transfers between devices, body(): lax.psum_scatter(grad_inner, 'shard', scatter_dimension=0, tiled=True)  432 us
    psum x1, waiting for transfers between devices, body(): lax.psum((owned[0], owned[1], owned[2], owned[3], owned[4], owned[5], own...  405 us
    all_gather x1, waiting for transfers between devices, body(): lax.all_gather(in_weight, 'shard', axis=0, tiled=True)  207 us
    dot_general x12, matrix products, span_step(): jnp.einsum('hts,shp->thp', decayed * scores[None], scaled_x, precision=HIGH)  192 us
    dot_general x16, matrix products, span_step(): jnp.einsum('tn,hpn->thp', readout, state, precision=HIGH)  80.2 us
    dot_general x12, matrix products, span_step(): jnp.einsum('sh,shp,sn->hpn', to_end, scaled_x, inputs_b, precision=HIGH)  65 us
    psum x1, blocking collectives, body(): lax.psum((owned[0], owned[1], owned[2], owned[3], owned[4], owned[5], own...  63.9 us
  transfers between devices with their start and end apart: 6, of which 3 were waited for; matrix products, arithmetic and copies ran while one was open for 57% of the time, Pallas kernels for 0%

commit v1 on v0

v1 whole, which is shorter than its diff:
```python
import functools

import jax
import jax.numpy as jnp
import numpy as np
from jax import lax
from jax.experimental import pallas as pl
from jax.experimental.pallas import tpu as pltpu
from jax.sharding import PartitionSpec as P

D = 1536
H = 48
HEADDIM = 64
N = 128
CONV = 4
DI = 3072
CW = 3328
XD = 3456
Q = 128
GW = 256
EPS = 1e-05
F32 = jnp.float32
BF = jnp.bfloat16
HIGH = lax.Precision.HIGHEST


def dot(a, b):
    return jnp.dot(a, b, preferred_element_type=F32)


def dot_nt(a, b):
    return lax.dot_general(a, b, (((1,), (1,)), ((), ())), preferred_element_type=F32)


def iota(shape, dim):
    return lax.broadcasted_iota(jnp.int32, shape, dim)


def sigmoid(v):
    return 0.5 * jnp.tanh(0.5 * v) + 0.5


def softplus(v):
    return jnp.maximum(v, 0.0) + jnp.log1p(jnp.exp(-jnp.abs(v)))


def params(limit):
    return pltpu.CompilerParams(
        dimension_semantics=("arbitrary",), vmem_limit_bytes=limit << 20
    )


def spread_consts():
    head_of = np.arange(DI) // HEADDIM
    ind = np.zeros((128, DI), np.float32)
    ind[head_of, np.arange(DI)] = 1
    ind[64 + head_of, np.arange(DI)] = 1
    wide = np.arange(H * Q) // Q
    ind2 = np.zeros((256, H * Q), np.float32)
    for at in (0, 64, 128):
        ind2[at + wide, np.arange(H * Q)] = 1
    ind_t = np.zeros((DI, 128), np.float32)
    ind_t[np.arange(DI), head_of] = 1
    rho_t = np.zeros((H * Q, 128), np.float32)
    rho_t[np.arange(H * Q), wide] = 1
    return [jnp.asarray(v, BF) for v in (ind, ind2, ind_t, rho_t)]


def prep_kernel(raw_ref, prm_ref, segc_ref, cum3_ref, ex_ref, cumt_ref):
    head = iota((Q, 128), 1) < H
    tri = (iota((Q, Q), 0) >= iota((Q, Q), 1)).astype(F32)
    bias = prm_ref[6:7, :128]
    rate = -jnp.exp(prm_ref[7:8, :128])

    def high(v):
        return v.astype(BF).astype(F32)

    def two(v):
        top = high(v)
        return (top + pltpu.roll(high(v - top), 64, axis=1)).astype(BF)

    for c in range(raw_ref.shape[0] // Q):
        rows = slice(c * Q, (c + 1) * Q)
        dt = jnp.where(head, softplus(raw_ref[rows, :] + bias), 0.0)
        cum = jnp.dot(tri, dt * rate, precision=HIGH, preferred_element_type=F32)
        cum = jnp.where(head, cum, 0.0)
        top = high(cum)
        mid = high(cum - top)
        low = high(cum - top - mid)
        cum3_ref[rows, :128] = (top + pltpu.roll(mid, 64, axis=1)).astype(BF)
        cum3_ref[rows, 128:] = low.astype(BF)
        carried = jnp.exp(cum) * segc_ref[rows, 4:5]
        to_end = jnp.exp(cum[Q - 1 : Q, :] - cum) * segc_ref[rows, 5:6]
        ex_ref[c, 0:Q, :] = two(dt)
        ex_ref[c, Q : 2 * Q, :] = two(jnp.where(head, carried, 0.0))
        ex_ref[c, 2 * Q :, :] = two(jnp.where(head, to_end, 0.0))
        cumt_ref[c] = cum.T[:H, :]


def prep(raw, prm, segc):
    tokens = raw.shape[0]
    chunks = tokens // Q
    return pl.pallas_call(
        prep_kernel,
        grid=(1,),
        in_specs=[
            pl.BlockSpec((tokens, 128), lambda i: (0, 0)),
            pl.BlockSpec((8, XD), lambda i: (0, 0)),
            pl.BlockSpec((tokens, 16), lambda i: (0, 0)),
        ],
        out_specs=[
            pl.BlockSpec((tokens, 256), lambda i: (0, 0)),
            pl.BlockSpec((chunks, 3 * Q, 128), lambda i: (0, 0, 0)),
            pl.BlockSpec((chunks, H, Q), lambda i: (0, 0, 0)),
        ],
        out_shape=[
            jax.ShapeDtypeStruct((tokens, 256), BF),
            jax.ShapeDtypeStruct((chunks, 3 * Q, 128), BF),
            jax.ShapeDtypeStruct((chunks, H, Q), F32),
        ],
        compiler_params=params(60),
        name="prep",
    )(raw, prm, segc)


VEC = 88


class Place:
    def __init__(self):
        self.rep, self.shard = lax.axis_index("rep"), lax.axis_index("shard")
        self.bits = lax.axis_size("rep").bit_length() - 1

    def bit(self, k):
        return (self.rep // (1 << k)) % 2

    def partner(self, k):
        if k == "x":
            return {"shard": 1 - self.shard}
        return {"rep": self.rep + (1 - 2 * self.bit(k)) * (1 << k)}

    def greet(self, keys):
        barrier = pltpu.get_barrier_semaphore()
        for k in keys:
            pl.semaphore_signal(
                barrier, inc=1, device_id=self.partner(k), device_id_type=pl.DeviceIdType.MESH
            )
        pl.semaphore_wait(barrier, len(keys))


class SemPool:
    def __init__(self, ref):
        self.ref, self.used = ref, 0

    def reserve(self, count):
        self.used += count
        return self.used - count


def in_two(ref):
    if len(ref.shape) > 2:
        return [ref.at[0], ref.at[1]] if ref.shape[0] == 2 else [ref]
    rows = ref.shape[0] // 2
    return [ref.at[pl.ds(0, rows)], ref.at[pl.ds(rows, rows)]] if rows % 16 == 0 else [ref]


def copiers(me, sems, base, count):
    sem = iter(range(count))
    at = lambda: sems.at[base + next(sem)]

    def remote(src, dst, key):
        return [
            pltpu.make_async_remote_copy(
                a, b, at(), at(), device_id=me.partner(key), device_id_type=pl.DeviceIdType.MESH
            )
            for a, b in zip(in_two(src), in_two(dst))
        ]

    def local(src, dst):
        return [pltpu.make_async_copy(src, dst, at())]

    return remote, local


class Chain:
    def claim(self, me, sems, name):
        self.me, self.sems, self.name = me, sems, name
        self.base = [sems.reserve(12) for _ in self.phases]

    def build(self, step):
        return self.copies(step, *copiers(self.me, self.sems.ref, self.base[step], 12))

    def start(self, step):
        for copy in self.build(step):
            copy.start()

    def finish(self, step):
        for copy in self.build(step):
            copy.wait()
        self.then(step)

    def then(self, step):
        pass


RATE = 0.085
HOP = 2.5


class Rows(Chain):
    def __init__(self, me, sems, name, src, full, low, count, order):
        self.src, self.full, self.rows, self.order = src, full, pl.ds(low, count), order
        self.size = 2 * 2 * count * full.shape[-1] / 1e6
        self.phases = ["x", order[0], order[1], "core"]
        self.claim(me, sems, name)

    def copies(self, step, remote, local):
        me, full = self.me, self.full
        b1, b2, core = me.bit(1), me.bit(2), me.bit(0)
        every = slice(None)
        at = {
            0: (b1, b2, core),
            1: (b1, b2, core),
            2: (every, b2, core) if self.order[0] == 1 else (b1, every, core),
            3: (every, every, core),
        }[step]
        part = full.at[at + (self.rows, every)]
        if step == 0:
            return remote(self.src((b1 * 2 + b2) * 2 + core), part, "x")
        return remote(part, part, 0 if step == 3 else self.order[step - 1])

    def cost(self, step):
        link = self.phases[step]
        if link == "core":
            return [(link, 4 * self.size / 2 / 0.2)]
        return [(link, (1, 1, 2)[step] * self.size / RATE)]


class Item(Chain):
    def __init__(
        self, me, sems, name, part, order, back, splits, shape, refs, src=None, dst=None, hand=None
    ):
        self.splits, self.shape = splits, shape
        self.order = list(order) + list(range(len(order), me.bits))
        self.back = [k for k in back if k <= splits]
        self.src, self.dst, self.hand = src, dst, hand
        self.keys = ["x"] + list(range(1, splits + 1))
        self.phases = []
        if part != "late":
            self.phases += self.order
        self.phases += {"early": ["store"], "late": ["load"], "all": []}[part]
        if part != "early":
            self.phases += [("back", k) for k in self.back] + ["out"]
        if refs is not None:
            self.bufs = self.take(refs, part)
        self.claim(me, sems, name)

    @staticmethod
    def shapes(bits, part, order, splits, shape):
        own = (2,) * splits
        out = [pltpu.VMEM(own + shape, BF)]
        if part == "late":
            return out
        out.append(pltpu.VMEM(own + shape, BF))
        free = splits + 1
        for k in list(order) + list(range(len(order), bits)):
            free -= k == "x" or k <= splits
            out.append(pltpu.VMEM((2,) * free + shape, BF))
        return out

    def take(self, refs, part):
        bufs = dict(all=refs.pop(0))
        if part != "late":
            bufs["acc"] = refs.pop(0)
            for k in self.order:
                bufs[k] = refs.pop(0)
        return bufs

    def own(self, key):
        return self.me.shard if key == "x" else self.me.bit(key)

    def place(self, done, key=None):
        out = []
        for k in self.keys:
            if k == self.order[0]:
                continue
            if k in done:
                out.append(self.own(k))
            else:
                out.append(1 - self.own(k) if k == key else slice(None))
        return tuple(out)

    def gathered(self, back):
        return tuple(
            slice(None) if k in back else self.own(k) for k in range(1, self.splits + 1)
        )

    def copies(self, step, remote, local):
        me, phase, bufs = self.me, self.phases[step], self.bufs
        if phase == "store":
            return local(bufs["all"].at[self.gathered(())], self.hand)
        if phase == "load":
            return local(self.hand, bufs["all"].at[self.gathered(())])
        if phase == "out":
            mine, dst = bufs["all"], self.dst(me.bit(0))
            return remote(mine, dst, 0) + local(mine, dst)
        if isinstance(phase, tuple):
            done = self.back[: self.back.index(phase[1])]
            part = bufs["all"].at[self.gathered(done)]
            return remote(part, part, phase[1])
        if step > 0:
            done = self.order[: self.order.index(phase)]
            return remote(bufs["acc"].at[self.place(done, phase)], bufs[phase], phase)
        every = (slice(None),) * self.splits
        if phase == "x":
            return remote(self.src(1 - me.shard, every), bufs["x"], "x") + local(
                self.src(me.shard, every), bufs["acc"]
            )
        out = []
        for s in range(2):
            at = lambda bit: tuple(
                bit if k == phase else slice(None) for k in range(1, self.splits + 1)
            )
            out += remote(self.src(s, at(1 - me.bit(phase))), bufs[phase].at[s], phase)
            out += local(self.src(s, at(me.bit(phase))), bufs["acc"].at[s])
        return out

    def then(self, step):
        phase, bufs = self.phases[step], self.bufs
        if phase in self.order:
            at = self.place(self.order[: self.order.index(phase) + 1])
            if phase == self.order[-1]:
                add_into(bufs["acc"], at, bufs[phase], bufs["all"], self.gathered(()))
            else:
                add_into(bufs["acc"], at, bufs[phase])

    def cost(self, step):
        phase = self.phases[step]
        piece = 2 * 2 * int(np.prod(self.shape)) / 1e6
        if phase == "out":
            return [("core", 2**self.splits * piece / 2 / 0.2)]
        if phase in ("store", "load"):
            return [("local" + self.name, 0.5)]
        if isinstance(phase, tuple):
            key = phase[1]
            pieces = 2 ** self.back.index(key)
        else:
            key = phase
            free = [k for k in self.order[self.order.index(key) + 1 :] if k in self.keys]
            pieces = 2 ** len(free)
        busy = pieces * piece / RATE
        if key == 3:
            return [(3, 2 * busy), (2, busy)]
        return [(key, busy)]


def add_into(acc, at, other, out=None, to=None):
    shape = other.shape
    rows = shape[-2]
    block = 48 if rows % 48 == 0 else 32
    lead = int(np.prod(shape[:-2], dtype=int))
    out, to = (acc, at) if out is None else (out, to)

    def fill(index, loop):
        loop = iter(loop)
        return tuple(next(loop) if isinstance(k, slice) else k for k in index)

    def step(i, _):
        place, low = i // (rows // block), (i % (rows // block)) * block
        loop = []
        for size in reversed(shape[:-2]):
            loop.insert(0, place % size)
            place = place // size
        last = (pl.ds(pl.multiple_of(low, block), block), slice(None))
        total = acc[fill(at, loop) + last] + other[tuple(loop) + last]
        out[fill(to, loop) + last] = total
        return 0

    lax.fori_loop(0, lead * (rows // block), step, 0)


def timeline(chains):
    free, events = {}, []
    ready = [(0.0, k, 0) for k in range(len(chains))]
    while ready:
        ready.sort()
        now, k, step = ready.pop(0)
        links = chains[k].cost(step)
        begin = max([now] + [free.get(link, 0.0) for link, _ in links])
        for link, busy in links:
            free[link] = begin + busy
        end = begin + max(busy for _, busy in links) + HOP
        events.append((max(now, begin - 2.0), len(events), "start", chains[k], step))
        events.append((end, len(events), "finish", chains[k], step))
        if step + 1 < len(chains[k].phases):
            ready.append((end, k, step + 1))
    return sorted(events, key=lambda e: (e[0], e[2] == "start", e[1]))


def run(events):
    for _, _, what, one, step in events:
        if what == "start":
            one.start(step)
        else:
            one.finish(step)


def by_tick(events, ticks, length):
    out = [[] for _ in range(ticks)]
    for event in events:
        out[min(int(np.ceil(event[0] / length)), ticks - 1)].append(event)
    return out


def run_tick(now, ticks):
    for at, events in enumerate(ticks):
        if events:

            @pl.when(now == at)
            def _():
                run(events)


def rep_bits():
    return lax.axis_size("rep").bit_length() - 1


def conv_at(buf, prm_ref, lanes, masks):
    taps = [buf[8 : 8 + Q, lanes]]
    for back in (1, 2, 3):
        taps.append(buf[8 - back : 8 - back + Q, lanes] * masks[back - 1])
    conv = prm_ref[4:5, lanes]
    for back in range(4):
        conv = conv + prm_ref[3 - back : 4 - back, lanes] * taps[back]
    return conv, taps


def halves(v):
    low = iota(v.shape, 1) < HEADDIM
    zero = jnp.zeros_like(v)
    return jnp.concatenate([jnp.where(low, v, zero), jnp.where(low, zero, v)], axis=0)


FWD_TICKS = 4


def fwd_kernel(
    xd_ref, segc_ref, segr_ref, cum3_ref, ex_ref, cumt_ref, prm_ref, ind_ref, ind2_ref,
    wt_ref, wo_ref,
    y_ref, sin_ref, conv_ref, wz_oth, wo_oth, buf, state, score, sems_ref,
):
    c = pl.program_id(0)
    chunks = pl.num_programs(0)
    me = Place()
    sems = SemPool(sems_ref)
    parts = []
    for k in range(3):
        order = (1, 2) if k % 2 else (2, 1)
        parts.append(
            Rows(
                me, sems, "z%d" % k,
                lambda piece, k=k: wt_ref.at[pl.ds(piece * 384 + k * 128, 128), :],
                wz_oth, k * 128, 128, order,
            )
        )
        parts.append(
            Rows(
                me, sems, "o%d" % k,
                lambda piece, k=k: wo_ref.at[pl.ds(piece * 192 + k * 64, 64), :],
                wo_oth, k * 64, 64, order[::-1],
            )
        )
    ticks = by_tick(timeline(parts), 8 * FWD_TICKS, 8.0 / FWD_TICKS)
    ending = ticks[-1]
    ticks[-1] = []

    @pl.when(c == 0)
    def _():
        me.greet(("x", 0, 1, 2))

    @pl.when(c == 0)
    def _():
        buf[0:8, :] = jnp.zeros((8, CW), F32)
        state[...] = jnp.zeros_like(state)

    @pl.when(c > 0)
    def _():
        buf[0:8, :] = buf[Q : Q + 8, :]

    buf[8:, :] = xd_ref[:, :CW]
    masks = [segc_ref[:, k : k + 1] for k in (1, 2, 3)]
    conv_bc, _ = conv_at(buf, prm_ref, slice(DI, CW), masks)
    conv_ref[:, DI:] = conv_bc
    bc = conv_bc * sigmoid(conv_bc)
    b_t = bc[:, :N].T.astype(BF)
    b_low = bc[:, :N].astype(BF)
    c_low = bc[:, N:].astype(BF)
    g = dot_nt(c_low, b_low)
    seen = (iota((Q, Q), 0) >= iota((Q, Q), 1)) & (segc_ref[:, 0:1] == segr_ref[0, 0:1, :])
    g = jnp.where(seen, g, 0.0)
    score[...] = jnp.concatenate([g, g], axis=1)

    def group(at, _):
        lanes = pl.ds(pl.multiple_of(at * GW, GW), GW)
        conv, _ = conv_at(buf, prm_ref, lanes, masks)
        conv_ref[:, lanes] = conv
        x = conv * sigmoid(conv)
        spread = dot(ex_ref[0], ind_ref[:, lanes])
        grown = spread[Q : 2 * Q]
        scaled = x * spread[:Q]
        now = state[:, lanes]
        now_low = now.astype(BF)
        sin_ref[0, :, lanes] = now_low
        y = dot(c_low, now_low) * grown + prm_ref[5:6, lanes] * x
        state[:, lanes] = grown[Q - 1 : Q, :] * now + dot(
            b_t, (scaled * spread[2 * Q :]).astype(BF)
        )
        parts = []
        for pair in range(2):
            wide = pl.ds(pl.multiple_of(at * 512 + pair * 256, 256), 256)
            column = dot(cum3_ref[...], ind2_ref[:, wide])
            head = at * 4 + pair * 2
            row = jnp.concatenate(
                [cumt_ref[0, pl.ds(head, 1), :], cumt_ref[0, pl.ds(head + 1, 1), :]], axis=1
            )
            mixed = jnp.exp(jnp.minimum(column - row, 0.0)) * score[...]
            values = halves(scaled[:, pair * 128 : (pair + 1) * 128]).astype(BF)
            parts.append(dot(mixed.astype(BF), values))
        y_ref[:, lanes] = y + jnp.concatenate(parts, axis=1)
        return 0

    def groups(place, _):
        run_tick(c * FWD_TICKS + place, ticks)
        for k in range(DI // GW // FWD_TICKS):
            group(place * (DI // GW // FWD_TICKS) + k, 0)
        return 0

    lax.fori_loop(0, FWD_TICKS, groups, 0)

    @pl.when(c == chunks - 1)
    def _():
        run(ending)


def scan_fwd(xd, segc, segr, cum3, ex, cumt, prm, ind, ind2, w_t, wo):
    hbm = pl.BlockSpec(memory_space=pl.ANY)
    tokens = xd.shape[0]
    chunks = tokens // Q
    fixed = lambda c: (0, 0)
    return pl.pallas_call(
        fwd_kernel,
        grid=(chunks,),
        in_specs=[
            pl.BlockSpec((Q, XD), lambda c: (c, 0)),
            pl.BlockSpec((Q, 16), lambda c: (c, 0)),
            pl.BlockSpec((1, 8, Q), lambda c: (c, 0, 0)),
            pl.BlockSpec((Q, 256), lambda c: (c, 0)),
            pl.BlockSpec((1, 3 * Q, 128), lambda c: (c, 0, 0)),
            pl.BlockSpec((1, H, Q), lambda c: (c, 0, 0)),
            pl.BlockSpec((8, XD), fixed),
            pl.BlockSpec((128, DI), fixed),
            pl.BlockSpec((256, H * Q), fixed),
            hbm,
            hbm,
        ],
        out_specs=[
            pl.BlockSpec((Q, DI), lambda c: (c, 0)),
            pl.BlockSpec((1, N, DI), lambda c: (c, 0, 0)),
            pl.BlockSpec((Q, CW), lambda c: (c, 0)),
            hbm,
            hbm,
        ],
        out_shape=[
            jax.ShapeDtypeStruct((tokens, DI), F32),
            jax.ShapeDtypeStruct((chunks, N, DI), BF),
            jax.ShapeDtypeStruct((tokens, CW), F32),
            jax.ShapeDtypeStruct((2, 2, 2, 384, D // 2), BF),
            jax.ShapeDtypeStruct((2, 2, 2, 192, D), BF),
        ],
        scratch_shapes=[
            pltpu.VMEM((Q + 8, CW), F32),
            pltpu.VMEM((N, DI), F32),
            pltpu.VMEM((Q, 2 * Q), F32),
            pltpu.SemaphoreType.DMA((320,)),
        ],
        compiler_params=pltpu.CompilerParams(
            dimension_semantics=("arbitrary",), collective_id=3, has_side_effects=True,
            vmem_limit_bytes=60 << 20,
        ),
        cost_estimate=pl.CostEstimate(
            flops=20_000_000_000, bytes_accessed=38_000_000, transcendentals=12_000_000
        ),
        name="scan_fwd",
    )(xd, segc, segr, cum3, ex, cumt, prm, ind, ind2, w_t, wo)


GT = 512


def owner_lanes(index, low, size, width):
    return pl.ds(pl.multiple_of(index * width + low, 128), size)


def gate_kernel(
    y_ref, nrm_ref, g_ref, u_ref, wz_own, wz_oth, wo_own, wo_oth, gain_ref,
    gn2_ref, dz2_ref, dz_ref, dy_ref, bo_ref, gg_ref, zs, dg, gn_held, dz_held, sems,
):
    rows = y_ref.shape[0]
    me = Place()
    shard = me.shard
    block, blocks = pl.program_id(0), pl.num_programs(0)
    half = DI // 2

    @pl.when(block == 0)
    def _():
        gg_ref[...] = jnp.zeros_like(gg_ref)
        me.greet((0,))

    def sent(block):
        remote, local = copiers(me, sems, block * 16, 16)
        slot = block % 2
        to = pl.ds(pl.multiple_of(block * rows, rows), rows)
        out = []
        for core, move in ((me.bit(0), None), (1 - me.bit(0), 0)):
            pairs = [(dz_held.at[slot, :, owner_lanes(core, 0, half, half)], dz2_ref, 0, half)]
            for s in range(2):
                low = s * half
                lanes = pl.ds(pl.multiple_of(core * (half // 2) + low, 128), half // 2)
                pairs.append((gn_held.at[slot, :, lanes], gn2_ref, s * (half // 2), half // 2))
            for src, both, low, width in pairs:
                if move is None:
                    out += local(src, both.at[0, to, pl.ds(low, width)])
                else:
                    dst = both.at[1, to, pl.ds(low, width)]
                    out += remote(src, dst, move)
        return out + local(dz_held.at[slot], dz_ref.at[to, :])

    @pl.when(block >= 2)
    def _():
        for copy in sent(block - 2):
            copy.wait()

    slot = block % 2

    def fold(v):
        return sum(v[:, k * 128 : (k + 1) * 128] for k in range(v.shape[1] // 128))

    nrm_own = owner_lanes(shard, 0, D // 2, D // 2)
    nrm_oth = owner_lanes(1 - shard, 0, D // 2, D // 2)
    squares = jnp.zeros((rows, 128), F32)
    moments = jnp.zeros((rows, 128), F32)
    for owner, wo in ((shard, wo_own), (1 - shard, wo_oth)):
        for at in range(DI // 2 // GT):
            lanes = owner_lanes(owner, at * GT, GT, DI // 2)
            z = dot_nt(nrm_ref[0, :, nrm_own], wz_own[lanes, :])
            z += dot_nt(nrm_ref[0, :, nrm_oth], wz_oth[lanes, :])
            d = dot_nt(g_ref[...], wo[at * GT : (at + 1) * GT, :]) * gain_ref[:, lanes]
            gated = y_ref[:, lanes] * (z * sigmoid(z))
            zs[:, lanes] = z
            dg[:, lanes] = d
            squares += fold(gated * gated)
            moments += fold(gated * d)
    r = lax.rsqrt(jnp.sum(squares, axis=1, keepdims=True) * (1.0 / DI) + EPS)
    k = r * r * r * (jnp.sum(moments, axis=1, keepdims=True) * (1.0 / DI))
    for at in range(DI // GT):
        lanes = slice(at * GT, (at + 1) * GT)
        z = zs[:, lanes]
        d = dg[:, lanes]
        y = y_ref[:, lanes]
        gain = gain_ref[:, lanes]
        sig = sigmoid(z)
        silu = z * sig
        gated = y * silu
        normal = gated * r
        gn_held[slot, :, lanes] = (normal * gain).astype(BF)
        d_gated = r * d - gated * k
        dy_ref[:, lanes] = (d_gated * silu).astype(BF)
        dz_held[slot, :, lanes] = (d_gated * y * (sig + silu * (1.0 - sig))).astype(BF)
        gg_ref[0:1, lanes] += jnp.sum(d * normal, axis=0, keepdims=True) / gain
    for copy in sent(block):
        copy.start()
    out = u_ref[...].astype(F32)
    for owner, wo in ((shard, wo_own), (1 - shard, wo_oth)):
        out += dot(gn_held[slot, :, owner_lanes(owner, 0, half, half)], wo[...])
    bo_ref[...] = out.astype(BF)

    @pl.when(block == blocks - 1)
    def _():
        for copy in sent(block - 1) + sent(block):
            copy.wait()


def gate(y, nrm, g, u, w_t, wz_oth, wo_own, wo_oth, gain):
    tokens = y.shape[0]
    rows = 256
    by_row = lambda i: (i, 0)
    fixed = lambda i: (0, 0)
    hbm = pl.BlockSpec(memory_space=pl.ANY)
    once = dict(pipeline_mode=pl.Buffered(1))
    return pl.pallas_call(
        gate_kernel,
        grid=(tokens // rows,),
        in_specs=[
            pl.BlockSpec((rows, DI), by_row),
            pl.BlockSpec((1, rows, D), lambda i: (0, i, 0)),
            pl.BlockSpec((rows, D), by_row),
            pl.BlockSpec((rows, D), by_row),
            pl.BlockSpec((DI, D // 2), fixed, **once),
            pl.BlockSpec((DI, D // 2), fixed, **once),
            pl.BlockSpec((DI // 2, D), fixed, **once),
            pl.BlockSpec((DI // 2, D), fixed, **once),
            pl.BlockSpec((1, DI), fixed),
        ],
        out_specs=[
            hbm,
            hbm,
            hbm,
            pl.BlockSpec((rows, DI), by_row),
            pl.BlockSpec((rows, D), by_row),
            pl.BlockSpec((8, DI), fixed),
        ],
        out_shape=[
            jax.ShapeDtypeStruct((2, tokens, DI // 2), BF),
            jax.ShapeDtypeStruct((2, tokens, DI // 2), BF),
            jax.ShapeDtypeStruct((tokens, DI), BF),
            jax.ShapeDtypeStruct((tokens, DI), BF),
            jax.ShapeDtypeStruct((tokens, D), BF),
            jax.ShapeDtypeStruct((8, DI), F32),
        ],
        scratch_shapes=[
            pltpu.VMEM((rows, DI), F32),
            pltpu.VMEM((rows, DI), F32),
            pltpu.VMEM((2, rows, DI), BF),
            pltpu.VMEM((2, rows, DI), BF),
            pltpu.SemaphoreType.DMA((16 * (tokens // rows),)),
        ],
        compiler_params=pltpu.CompilerParams(
            dimension_semantics=("arbitrary",), collective_id=4, has_side_effects=True,
            vmem_limit_bytes=60 << 20,
        ),
        cost_estimate=pl.CostEstimate(
            flops=29_000_000_000, bytes_accessed=64_000_000, transcendentals=6_000_000
        ),
        name="gate",
    )(y, nrm, g, u, w_t, wz_oth, wo_own, wo_oth, gain)


def widen_kernel(gz0_ref, gz1_ref, gx_ref, gb_ref, go0_ref, go1_ref, inner_ref, outer_ref):
    at = pl.program_id(0)
    first, outer_first = to_end("gz") // 2, to_end("go")

    def fill(when, out, ref):
        @pl.when(when)
        def _():
            out[...] = ref[...].astype(F32)

    fill((at < 4) & (at % 2 < first), inner_ref, gz0_ref)
    fill((at < 4) & (at % 2 >= first), inner_ref, gz1_ref)
    fill((at >= 4) & (at < 8), inner_ref, gx_ref)
    fill((at < 6) & (at % 3 < outer_first), outer_ref, go0_ref)
    fill((at < 6) & (at % 3 >= outer_first), outer_ref, go1_ref)

    @pl.when(at == 8)
    def _():
        inner_ref[:384, :] = gb_ref[...].astype(F32)


def widen(gz0, gz1, gx, gb, go0, go1):
    half = D // 2

    def rows(height, cols, low, high, each, base=0):
        def at(i):
            i = jnp.clip(i - base, 0, 2 * each - 1)
            return ((i // each) * (high - low) + jnp.clip(i % each - low, 0, high - low - 1), 0)

        return pl.BlockSpec((height, cols), at)

    first, outer_first = to_end("gz") // 2, to_end("go")
    assert to_end("gz") == 2
    return pl.pallas_call(
        widen_kernel,
        grid=(9,),
        in_specs=[
            rows(768, half, 0, first, 2), rows(768, half, first, 2, 2), rows(768, half, 0, 2, 2, 4),
            pl.BlockSpec((384, half), lambda i: (0, 0)),
            rows(256, D, 0, outer_first, 3), rows(256, D, outer_first, 3, 3),
        ],
        out_specs=[
            pl.BlockSpec((768, half), lambda i: (i, 0)),
            pl.BlockSpec((256, D), lambda i: (jnp.minimum(i, 5), 0)),
        ],
        out_shape=[
            jax.ShapeDtypeStruct((CW + DI + H, half), F32),
            jax.ShapeDtypeStruct((DI // 2, D), F32),
        ],
        compiler_params=params(60),
        cost_estimate=pl.CostEstimate(flops=0, bytes_accessed=44_000_000, transcendentals=0),
        name="widen",
    )(
        gz0.reshape(-1, half), gz1.reshape(-1, half), gx.reshape(-1, half), gb.reshape(-1, half),
        go0.reshape(-1, D), go1.reshape(-1, D),
    )


BWD_TICKS = 4


def bwd_kernel(
    bits,
    xd_ref, conv_ref, dy_ref, sin_ref, segc_ref, segr_ref, cum3_ref, ex_ref, cumt_ref, prm_ref,
    ind_ref, ind2_ref, ind_t_ref, rho_t_ref, go, gz,
    dxd_ref, dx2_ref, pg_ref, go_hand, gz_hand, go_out, gz_out,
    dbuf, dstate, score, d_score, d_b, d_c, rho, red, gam, kept, held, pair_sems, *rest,
):
    c = pl.program_id(0)
    chunks = pl.num_programs(0)
    me = Place()
    slot = c % 2

    def sent(c):
        remote, local = copiers(me, pair_sems, c * 12, 12)
        mine = held.at[c % 2]
        to = pl.ds(pl.multiple_of((chunks - 1 - c) * Q, Q), Q)
        lanes = lambda core: owner_lanes(core, 0, DI // 2, DI // 2)
        tail = mine.at[:, pl.ds(DI, XD - DI)]
        half, rest = pl.ds(0, DI // 2), pl.ds(DI // 2, XD - DI)
        return (
            remote(mine.at[:, lanes(1 - me.bit(0))], dx2_ref.at[1, to, half], 0)
            + remote(tail, dx2_ref.at[1, to, rest], 0)
            + local(mine.at[:, lanes(me.bit(0))], dx2_ref.at[0, to, half])
            + local(tail, dx2_ref.at[0, to, rest])
            + local(mine, dxd_ref.at[to, :])
        )

    @pl.when(c >= 2)
    def _():
        for copy in sent(c - 2):
            copy.wait()

    items = plan_items(
        me, SemPool(rest[-1]), list(rest[:-1]), early_plan(), dict(go=go, gz=gz),
        dict(go=(go_out, 0), gz=(gz_out, 0)), dict(go=go_hand, gz=gz_hand),
    )
    ticks = by_tick(timeline(items), 8 * BWD_TICKS, 14.4 / BWD_TICKS)
    ending = ticks[-1]
    ticks[-1] = []

    @pl.when(c == 0)
    def _():
        me.greet(("x",) + tuple(range(bits)))

    @pl.when(c == 0)
    def _():
        dbuf[Q:, :] = jnp.zeros((8, CW), F32)
        dstate[...] = jnp.zeros_like(dstate)
        pg_ref[...] = jnp.zeros_like(pg_ref)

    @pl.when(c > 0)
    def _():
        dbuf[Q:, :] = dbuf[0:8, :]

    masks_next = [segc_ref[:, k : k + 1] for k in (6, 7, 8)]

    def conv_back(lanes, d_conv):
        dbuf[0:Q, lanes] = d_conv
        raw = xd_ref[:, lanes]
        moved = d_conv
        total = 0.0
        for ahead in range(4):
            if ahead:
                moved = dbuf[ahead : ahead + Q, lanes] * masks_next[ahead - 1]
            total += prm_ref[3 - ahead : 4 - ahead, lanes] * moved
            pg_ref[3 - ahead : 4 - ahead, lanes] += jnp.sum(moved * raw, axis=0, keepdims=True)
        held[slot, :, lanes] = total.astype(BF)
        pg_ref[4:5, lanes] += jnp.sum(d_conv, axis=0, keepdims=True)

    conv_bc = conv_ref[:, DI:]
    sig_bc = sigmoid(conv_bc)
    bc = conv_bc * sig_bc
    c_t = bc[:, N:].T.astype(BF)
    b_low = bc[:, :N].astype(BF)
    c_low = bc[:, N:].astype(BF)
    g = dot_nt(b_low, c_low)
    seen = (iota((Q, Q), 0) <= iota((Q, Q), 1)) & (segc_ref[:, 0:1] == segr_ref[0, 0:1, :])
    g = jnp.where(seen, g, 0.0)
    score[...] = jnp.concatenate([g, g], axis=1)
    d_score[...] = jnp.zeros_like(d_score)
    d_b[...] = jnp.zeros_like(d_b)
    d_c[...] = jnp.zeros_like(d_c)
    rho[...] = jnp.zeros_like(rho)
    red[...] = jnp.zeros_like(red)

    def group(at, _):
        lanes = pl.ds(pl.multiple_of(at * GW, GW), GW)
        conv = conv_ref[:, lanes]
        sig = sigmoid(conv)
        x = conv * sig
        spread = dot(ex_ref[0], ind_ref[:, lanes])
        step = spread[:Q]
        grown = spread[Q : 2 * Q]
        to_end = spread[2 * Q :]
        scaled = x * step
        dy_low = dy_ref[:, lanes]
        dy = dy_low.astype(F32)
        dy_grown = (dy * grown).astype(BF)
        s_in = sin_ref[0, :, lanes]
        ds = dstate[:, lanes]
        ds_low = ds.astype(BF)
        carried = dy * (dot(c_low, s_in) * grown)
        d_left = dot(b_low, ds_low) * to_end
        leaving = scaled * d_left
        d_c[...] += dot_nt(dy_grown, s_in)
        d_b[...] += dot_nt((scaled * to_end).astype(BF), ds_low)
        kept_row = grown[Q - 1 : Q, :]
        kept[0:1, lanes] = kept_row * jnp.sum(s_in.astype(F32) * ds, axis=0, keepdims=True)
        dstate[:, lanes] = kept_row * ds + dot(c_t, dy_grown)
        parts = []
        for pair in range(2):
            own = slice(pair * 128, (pair + 1) * 128)
            wide = pl.ds(pl.multiple_of(at * 512 + pair * 256, 256), 256)
            column = dot(cum3_ref[...], ind2_ref[:, wide])
            head = at * 4 + pair * 2
            row = jnp.concatenate(
                [cumt_ref[0, pl.ds(head, 1), :], cumt_ref[0, pl.ds(head + 1, 1), :]], axis=1
            )
            decay = jnp.exp(jnp.minimum(row - column, 0.0))
            values = halves(dy_low[:, own])
            d_mixed = dot_nt(scaled[:, own].astype(BF), values) * decay
            d_score[...] += d_mixed[:, :Q] + d_mixed[:, Q:]
            through = score[...]
            parts.append(dot((decay * through).astype(BF), values))
            change = (d_mixed * through).astype(BF)
            rho[...] += dot(change, rho_t_ref[wide, :])
            sums = jnp.sum(change.astype(F32), axis=0, keepdims=True)
            gam[pl.ds(head, 1), :] = sums[:, :Q]
            gam[pl.ds(head + 1, 1), :] = sums[:, Q:]
        d_scaled = jnp.concatenate(parts, axis=1) + d_left
        red[...] += dot(
            jnp.concatenate([carried, leaving, d_scaled * x], axis=0).astype(BF),
            ind_t_ref[lanes, :],
        )
        pg_ref[5:6, lanes] += jnp.sum(dy * x, axis=0, keepdims=True)
        d_x = d_scaled * step + prm_ref[5:6, lanes] * dy
        conv_back(lanes, d_x * (sig + x * (1.0 - sig)))
        return 0

    def groups(place, _):
        run_tick(c * BWD_TICKS + place, ticks)
        for k in range(DI // GW // BWD_TICKS):
            group(place * (DI // GW // BWD_TICKS) + k, 0)
        return 0

    lax.fori_loop(0, BWD_TICKS, groups, 0)

    d_score[...] = jnp.where(seen, d_score[...], 0.0)
    ds_low = d_score[...].astype(BF)
    d_b_all = d_b[...] + dot(ds_low, c_low)
    d_c_all = d_c[...] + dot(d_score[...].T.astype(BF), b_low)
    d_bc = jnp.concatenate([d_b_all, d_c_all], axis=1)
    conv_back(slice(DI, CW), d_bc * (sig_bc + bc * (1.0 - sig_bc)))

    kept_all = jnp.broadcast_to(kept[0:1, :], (16, DI))
    kept_high = kept_all.astype(BF)
    kept_low = (kept_all - kept_high.astype(F32)).astype(BF)
    kept_sum = (dot(kept_high, ind_t_ref[...]) + dot(kept_low, ind_t_ref[...]))[0:1, :]
    gam_t = jnp.concatenate([gam[...], jnp.zeros((128 - H, Q), F32)], axis=0).T
    after = (iota((Q, Q), 0) <= iota((Q, Q), 1)).astype(F32)
    before = (iota((Q, Q), 0) > iota((Q, Q), 1)).astype(F32)
    d_log = (
        jnp.dot(after, red[0:Q, :] + gam_t - rho[...], precision=HIGH, preferred_element_type=F32)
        + jnp.dot(before, red[Q : 2 * Q, :], precision=HIGH, preferred_element_type=F32)
        + kept_sum
    )
    head = iota((Q, 128), 1) < H
    value = xd_ref[:, CW:] + prm_ref[6:7, :128]
    rate = -jnp.exp(prm_ref[7:8, :128])
    d_raw = jnp.where(head, (red[2 * Q :, :] + d_log * rate) * sigmoid(value), 0.0)
    held[slot, :, CW:] = d_raw.astype(BF)
    for copy in sent(c):
        copy.start()
    pg_ref[6:7, :128] += jnp.sum(d_raw, axis=0, keepdims=True)
    pg_ref[7:8, :128] += jnp.sum(
        jnp.where(head, d_log * rate * softplus(value), 0.0), axis=0, keepdims=True
    )

    @pl.when(c == chunks - 1)
    def _():
        run(ending)
        for copy in sent(c - 1) + sent(c):
            copy.wait()


def scan_bwd(xd, conv, dy, sin, segc, segr, cum3, ex, cumt, prm, ind, ind2, ind_t, rho_t, go, gz):
    tokens = xd.shape[0]
    bits = rep_bits()
    hbm = pl.BlockSpec(memory_space=pl.ANY)
    chunks = tokens // Q
    fixed = lambda c: (0, 0)
    back = lambda c: (chunks - 1 - c, 0)
    back3 = lambda c: (chunks - 1 - c, 0, 0)
    once = dict(pipeline_mode=pl.Buffered(1))
    return pl.pallas_call(
        functools.partial(bwd_kernel, bits),
        grid=(chunks,),
        in_specs=[
            pl.BlockSpec((Q, XD), back),
            pl.BlockSpec((Q, CW), back),
            pl.BlockSpec((Q, DI), back),
            pl.BlockSpec((1, N, DI), back3),
            pl.BlockSpec((Q, 16), back),
            pl.BlockSpec((1, 8, Q), back3),
            pl.BlockSpec((Q, 256), back),
            pl.BlockSpec((1, 3 * Q, 128), back3),
            pl.BlockSpec((1, H, Q), back3),
            pl.BlockSpec((8, XD), fixed),
            pl.BlockSpec((128, DI), fixed, **once),
            pl.BlockSpec((256, H * Q), fixed, **once),
            pl.BlockSpec((DI, 128), fixed, **once),
            pl.BlockSpec((H * Q, 128), fixed, **once),
            hbm,
            hbm,
        ],
        out_specs=[hbm] * 2 + [pl.BlockSpec((8, XD), fixed)] + [hbm] * 4,
        out_shape=[
            jax.ShapeDtypeStruct((tokens, XD), BF),
            jax.ShapeDtypeStruct((2, tokens, XD - DI // 2), BF),
            jax.ShapeDtypeStruct((8, XD), F32),
            part_array("go", 3 - to_end("go"), sent=True),
            part_array("gz", 4 - to_end("gz"), sent=True),
            part_array("go", to_end("go")),
            part_array("gz", to_end("gz")),
        ],
        scratch_shapes=[
            pltpu.VMEM((Q + 8, CW), F32),
            pltpu.VMEM((N, DI), F32),
            pltpu.VMEM((Q, 2 * Q), F32),
            pltpu.VMEM((Q, Q), F32),
            pltpu.VMEM((Q, N), F32),
            pltpu.VMEM((Q, N), F32),
            pltpu.VMEM((Q, 128), F32),
            pltpu.VMEM((3 * Q, 128), F32),
            pltpu.VMEM((H, Q), F32),
            pltpu.VMEM((8, DI), F32),
            pltpu.VMEM((2, Q, XD), BF),
            pltpu.SemaphoreType.DMA((12 * chunks,)),
            *plan_scratch(bits, early_plan()),
            pltpu.SemaphoreType.DMA((1024,)),
        ],
        compiler_params=pltpu.CompilerParams(
            dimension_semantics=("arbitrary",), collective_id=1, has_side_effects=True,
            vmem_limit_bytes=60 << 20,
        ),
        cost_estimate=pl.CostEstimate(
            flops=60_000_000_000, bytes_accessed=50_000_000, transcendentals=18_000_000
        ),
        name="scan_bwd",
    )(
        xd, conv, dy, sin, segc, segr, cum3, ex, cumt, prm, ind, ind2, ind_t, rho_t,
        in_parts("go", go), in_parts("gz", gz),
    )


def gather_kernel(
    u_ref, vec_ref, wt_ref, wb_ref, g_ref,
    wx_oth, wb_oth, vec2_ref, nrm2_ref, g2_ref, raw_ref, xd_ref,
    gain, weights, arrived, acc, nrm_ref, g_held, sems_ref,
):
    me = Place()
    s = me.shard
    sems = SemPool(sems_ref)
    tokens = u_ref.shape[0]
    half = D // 2
    own = pl.ds(pl.multiple_of(s * half, half), half)
    oth = pl.ds(pl.multiple_of((1 - s) * half, half), half)
    parts = []
    for k, order in enumerate(((1, 2), (2, 1), (1, 2))):
        parts.append(
            Rows(
                me, sems, "x%d" % k,
                lambda piece, k=k: wt_ref.at[pl.ds(DI + piece * 384 + k * 128, 128), :],
                wx_oth, k * 128, 128, order,
            )
        )
    parts.append(
        Rows(
            me, sems, "b", lambda piece: wb_ref.at[pl.ds(piece * 48, 48), :], wb_oth, 0, 48, (2, 1)
        )
    )
    at = sems.reserve(24)
    pairs = sems.reserve(16)
    me.greet(("x", 0, 1, 2))
    swap = pltpu.make_async_remote_copy(
        vec_ref, vec2_ref.at[s], sems_ref.at[at], sems_ref.at[at + 1], device_id=me.partner("x"),
        device_id_type=pl.DeviceIdType.MESH,
    )
    swap.start()
    for part in parts:
        part.start(0)
    loads = [
        (vec_ref, vec2_ref.at[s]),
        (wt_ref.at[pl.ds(DI, DI), :], weights.at[pl.ds(0, DI), :]),
        (wb_ref, weights.at[pl.ds(DI, 384), :]),
    ]
    loads = [pltpu.make_async_copy(*v, sems_ref.at[at + 2 + k]) for k, v in enumerate(loads)]
    for copy in loads:
        copy.start()
    fetch = pltpu.make_async_copy(g_ref, g_held, sems_ref.at[pairs])
    fetch.start()

    def share(held, both, base):
        remote, local = copiers(me, sems_ref, base, 5)
        return remote(held, both.at[1], 0) + local(held, both.at[0])

    swap.wait()
    loads[0].wait()
    fetch.wait()
    shared = share(g_held, g2_ref, pairs + 1)
    for copy in shared:
        copy.start()
    for shard in range(2):
        for k in range(half // 128):
            low = shard * half + k * 128
            gain[0:1, low : low + 128] = vec2_ref[shard, k : k + 1, :]

    def norm(at, _):
        rows = pl.ds(pl.multiple_of(at * 128, 128), 128)
        u = u_ref[rows, :].astype(F32)
        q = lax.rsqrt(jnp.sum(u * u, axis=1, keepdims=True) * (1.0 / D) + EPS)
        nrm_ref[rows, :] = (u * q * gain[...]).astype(BF)
        return 0

    lax.fori_loop(0, tokens // 128, norm, 0)
    later = share(nrm_ref, nrm2_ref, pairs + 6)
    for copy in later:
        copy.start()
    loads[1].wait()
    loads[2].wait()

    def by_rows(body):
        body(slice(0, tokens))

    def first(low):
        def body(rows):
            acc[rows, low : low + 384] = dot_nt(nrm_ref[rows, own], weights[low : low + 384, :])

        by_rows(body)

    def arrive(k):
        source = wx_oth.at[:, :, :, pl.ds(k * 128, 128), :]
        return pltpu.make_async_copy(source, arrived.at[k], sems_ref.at[at + 8 + k])

    def second(k, piece):
        if piece == 0:
            arrive(k).wait()
        low = piece * 384 + k * 128

        def body(rows):
            acc[rows, low : low + 128] += dot_nt(
                nrm_ref[rows, oth], arrived[k, piece // 4, (piece // 2) % 2, piece % 2]
            )

        by_rows(body)

    events = [e for e in timeline(parts) if not (e[2] == "start" and e[4] == 0)]
    work = [(1.3, functools.partial(first, low)) for low in range(0, XD, 384)]
    now = 8.0
    while events or work:
        if work and (not events or events[0][0] > now + 0.5):
            long, task = work.pop(0)
            task()
            now += long
            continue
        event = events.pop(0)
        run([event])
        now = max(now, event[0])
        _, _, what, part, step = event
        k = parts.index(part)
        if what == "finish" and step == 3 and k < 3:
            arrive(k).start()
            work += [(0.6, functools.partial(second, k, piece)) for piece in range(8)]
    loads = []
    for k in range(8):
        source = wb_oth.at[k // 4, (k // 2) % 2, k % 2]
        target = weights.at[pl.ds(k * 48, 48), :]
        loads.append(pltpu.make_async_copy(source, target, sems_ref.at[at + 16 + k]))
    for copy in loads:
        copy.start()
    for copy in loads:
        copy.wait()

    def last(at, _):
        rows = pl.ds(pl.multiple_of(at * 256, 256), 256)
        acc[rows, DI:] += dot_nt(nrm_ref[rows, oth], weights[:384, :])
        return 0

    lax.fori_loop(0, tokens // 256, last, 0)
    out = pltpu.make_async_copy(acc, xd_ref, sems_ref.at[at + 13])
    out.start()
    raw_ref[...] = acc[:, CW:]
    for copy in shared + later:
        copy.wait()
    out.wait()


def gather(u, vec, wt, wb, g):
    tokens = u.shape[0]
    vmem = pl.BlockSpec(memory_space=pltpu.VMEM)
    hbm = pl.BlockSpec(memory_space=pl.ANY)
    sds = jax.ShapeDtypeStruct
    return pl.pallas_call(
        gather_kernel,
        in_specs=[vmem, vmem, hbm, hbm, hbm],
        out_specs=[hbm, hbm, vmem, hbm, hbm, vmem, hbm],
        out_shape=[
            sds((2, 2, 2, 384, D // 2), BF),
            sds((2, 2, 2, 48, D // 2), BF),
            sds((2, VEC, 128), F32),
            sds((2, tokens, D), BF),
            sds((2, tokens, D), BF),
            sds((tokens, 128), F32),
            sds((tokens, XD), F32),
        ],
        scratch_shapes=[
            pltpu.VMEM((1, D), F32),
            pltpu.VMEM((XD, D // 2), BF),
            pltpu.VMEM((3, 2, 2, 2, 128, D // 2), BF),
            pltpu.VMEM((tokens, XD), F32),
            pltpu.VMEM((tokens, D), BF),
            pltpu.VMEM((tokens, D), BF),
            pltpu.SemaphoreType.DMA((256,)),
        ],
        compiler_params=pltpu.CompilerParams(
            collective_id=0, has_side_effects=True, vmem_limit_bytes=60 << 20
        ),
        cost_estimate=pl.CostEstimate(
            flops=11_000_000_000, bytes_accessed=40_000_000, transcendentals=1024
        ),
        name="gather",
    )(u, vec, wt, wb, g)


TAIL_ROWS = 256
TAIL_PLACES = 6

EARLY = [
    ("go", 1, (1, 2, "x", 3), (3, 1, 2), False),
    ("gz", 1, ("x", 1, 2, 3), (3, 2, 1), True),
    ("go", 0, ("x", 1, 2, 3), (2, 3, 1), True),
    ("gz", 0, ("x", 1, 2, 3), (2, 3, 1), True),
    ("go", 2, ("x", 1, 2, 3), (3, 1, 2), False),
    ("gz", 2, (2, 1, "x", 3), (3, 2, 1), False),
    ("gz", 3, (2, "x", 1, 3), (1, 2, 3), False),
]
LATE = [
    ("gz", 2, ("x", 1, 2, 3), (2, 3, 1)),
    ("gx", 2, (2, 1, "x", 3), (1, 3, 2)),
    ("gx", 3, ("x", 1, 2, 3), (3, 2, 1)),
    ("gx", 0, ("x", 1, 2, 3), (3, 1, 2)),
    ("gb", 0, ("x", 1, 2, 3), (3, 2, 1)),
    ("gx", 1, (1, "x", 2, 3), (2, 3, 1)),
    ("go", 2, ("x", 1, 2, 3), (3, 2, 1)),
    ("go", 1, ("x", 1, 2, 3), (2, 3, 1)),
    ("gz", 3, (1, "x", 2, 3), (3, 2, 1)),
]
KINDS = dict(
    go=(3, 3, 32, D), gz=(4, 3, 48, D // 2), gx=(4, 3, 48, D // 2), gb=(1, 2, 48, D // 2)
)


def to_end(kind):
    return sum(1 for k, _, _, _, full in EARLY if k == kind and full)


def early_plan():
    return [(k, n, "all" if full else "early", o, back) for k, n, o, back, full in EARLY]


def tail_plan():
    return [
        (k, n, "all" if k in ("gx", "gb") else "late", order, back) for k, n, order, back in LATE
    ]


def plan_scratch(bits, plan):
    out = []
    for kind, _, part, order, _ in plan:
        _, splits, rows, cols = KINDS[kind]
        out += Item.shapes(bits, part, order, splits, (rows, cols))
    return out


def plan_items(me, sems, refs, plan, grads, outs, hands):
    half = D // 2
    items = []
    for kind, n, part, order, back in plan:
        _, splits, rows, cols = KINDS[kind]
        grad, (out, first), hand = grads.get(kind), outs.get(kind, (None, 0)), None
        if part != "all":
            hand = hands[kind].at[n - to_end(kind)]
        if kind == "go":
            src = lambda s, at, grad=grad, n=n: grad.at[(s, n) + at]
        else:
            lead = (n,) if kind != "gb" else (4, me.bit(0))
            src = lambda s, at, grad=grad, lead=lead: grad.at[
                lead + at + (slice(None), pl.ds(pl.multiple_of(s * half, half), half))
            ]
        dst = lambda core, out=out, at=n - first: out.at[core, at]
        items.append(
            Item(
                me, sems, kind + str(n), part, order, back, splits, (rows, cols), refs, src, dst, hand
            )
        )
    return items


def part_array(kind, count, sent=False):
    _, splits, rows, cols = KINDS[kind]
    lead = (count,) if sent else (2, count) + (2,) * splits
    return jax.ShapeDtypeStruct(lead + (rows, cols), BF)


def in_parts(kind, grad):
    parts, splits, rows, _ = KINDS[kind]
    lead = (2, parts) if kind == "go" else (parts,)
    return grad.reshape(lead + (2,) * splits + (rows, D))


def tail_kernel(
    bits,
    dz_ref, dxd_ref, u_ref, g_ref, gain_ref, w_own, wb_own, wz_oth, wx_oth, wb_oth,
    go_hand, gz_hand, gx, small,
    out_ref, gg_out, go_out, gz_out, gx_out, gb_out, small_out,
    wz0, wx0, wb0, wz1, wx1, wb1, gg, dn, sm_send, sm_sum, sm_recv, *rest,
):
    c = pl.program_id(0)
    steps = pl.num_programs(0)
    rest, sem_ref = list(rest[:-1]), rest[-1]
    me = Place()
    sems = SemPool(sem_ref)
    half = D // 2
    loads = [
        (w_own.at[pl.ds(0, DI), :], wz0), (w_own.at[pl.ds(DI, DI), :], wx0), (wb_own, wb0),
        (wz_oth, wz1), (wx_oth, wx1), (wb_oth, wb1),
    ]
    load_base = sems.reserve(len(loads))

    def load(k):
        return pltpu.make_async_copy(*loads[k], sem_ref.at[load_base + k])

    items = plan_items(
        me, sems, rest, tail_plan(), dict(gx=gx, gb=gx),
        dict(go=(go_out, to_end("go")), gz=(gz_out, to_end("gz")), gx=(gx_out, 0), gb=(gb_out, 0)),
        dict(go=go_hand, gz=gz_hand),
    )
    ticks = by_tick(timeline(items), 4 * TAIL_PLACES, 10.4 / TAIL_PLACES)
    ending = ticks[-1]
    ticks[-1] = []

    @pl.when(c == 0)
    def _():
        gg[...] = jnp.zeros_like(gg)
        me.greet(("x",) + tuple(range(bits)))
        for k in range(len(loads)):
            load(k).start()

    shard = me.shard
    place = 0
    for part, (owner, wz, wx, wb) in enumerate(
        [(shard, wz0, wx0, wb0), (1 - shard, wz1, wx1, wb1)]
    ):
        for low in range(0, half, 256):
            run_tick(c * TAIL_PLACES + place, ticks)
            place += 1
            if low == 0:

                @pl.when(c == 0)
                def _():
                    for k in range(3 * part, 3 * part + 3):
                        load(k).wait()

            lanes = owner_lanes(owner, low, 256, half)
            own = slice(low, low + 256)
            total = dot(dz_ref[...], wz[:, own]) + dot(dxd_ref[:, :DI], wx[:, own])
            dn[:, lanes] = total + dot(dxd_ref[:, DI:], wb[:, own])
    u = u_ref[...].astype(F32)
    d = dn[...]
    q = lax.rsqrt(jnp.sum(u * u, axis=1, keepdims=True) * (1.0 / D) + EPS)
    scaled = d * gain_ref[...]
    mean = jnp.sum(scaled * u, axis=1, keepdims=True) * (1.0 / D)
    out_ref[...] = g_ref[...].astype(F32) + q * scaled - u * (q * q * q * mean)
    gg[0:1, :] += jnp.sum(d * u * q, axis=0, keepdims=True)

    @pl.when(c == steps - 1)
    def _():
        base = sems.reserve(2 * (bits + 1))
        for s in range(2):
            sm_send[s] = small[s]
            for k in range(half // 128):
                low = s * half + k * 128
                sm_send[s, k : k + 1, :] = gg[0:1, low : low + 128]

        def swap(k):
            if k == 0:
                src, key = sm_send.at[1 - me.shard], "x"
            else:
                src, key = sm_sum, k - 1
            return pltpu.make_async_remote_copy(
                src, sm_recv.at[k], sem_ref.at[base + 2 * k], sem_ref.at[base + 2 * k + 1],
                device_id=me.partner(key), device_id_type=pl.DeviceIdType.MESH,
            )

        swap(0).start()
        events = ending
        share = -(-len(events) // (bits + 2))
        for k in range(bits + 1):
            run(events[k * share : (k + 1) * share])
            swap(k).wait()
            if k == 0:
                sm_sum[...] = sm_send[me.shard] + sm_recv[0]
            else:
                sm_sum[...] += sm_recv[k]
            if k < bits:
                swap(k + 1).start()
        run(events[(bits + 1) * share :])
        small_out[...] = sm_sum[...]


def tail(dz, dxd, u, g, gain, w_t, wb_own, wz_oth, wx_oth, wb_oth, go_hand, gz_hand, gx, small):
    bits = rep_bits()
    tokens = dz.shape[0]
    rows = TAIL_ROWS
    by_row = lambda i: (i, 0)
    fixed = lambda i: (0, 0)
    hbm = pl.BlockSpec(memory_space=pl.ANY)
    sds = jax.ShapeDtypeStruct
    half = D // 2
    scratch = []
    for height in (DI, DI, 384, DI, DI, 384):
        scratch.append(pltpu.VMEM((height, half), BF))
    scratch += [
        pltpu.VMEM((8, D), F32),
        pltpu.VMEM((rows, D), F32),
        pltpu.VMEM((2, VEC, 128), F32),
        pltpu.VMEM((VEC, 128), F32),
        pltpu.VMEM((bits + 1, VEC, 128), F32),
    ]
    scratch += plan_scratch(bits, tail_plan())
    scratch.append(pltpu.SemaphoreType.DMA((1400,)))
    return pl.pallas_call(
        functools.partial(tail_kernel, bits),
        grid=(tokens // rows,),
        in_specs=[
            pl.BlockSpec((rows, DI), by_row),
            pl.BlockSpec((rows, XD), by_row),
            pl.BlockSpec((rows, D), by_row),
            pl.BlockSpec((rows, D), by_row),
            pl.BlockSpec((1, D), fixed),
        ]
        + [hbm] * 8
        + [pl.BlockSpec((2, VEC, 128), lambda i: (0, 0, 0))],
        out_specs=[
            pl.BlockSpec((rows, D), by_row),
            pl.BlockSpec((8, D), fixed),
            hbm, hbm, hbm, hbm,
            pl.BlockSpec((VEC, 128), fixed),
        ],
        out_shape=[
            sds((tokens, D), F32),
            sds((8, D), F32),
            part_array("go", 3 - to_end("go")),
            part_array("gz", 4 - to_end("gz")),
            part_array("gx", 4),
            part_array("gb", 1),
            sds((VEC, 128), F32),
        ],
        scratch_shapes=scratch,
        compiler_params=pltpu.CompilerParams(
            dimension_semantics=("arbitrary",), collective_id=2, has_side_effects=True,
            vmem_limit_bytes=62 << 20,
        ),
        cost_estimate=pl.CostEstimate(
            flops=20_500_000_000, bytes_accessed=80_000_000, transcendentals=1024
        ),
        name="tail",
    )(
        dz, dxd, u, g, gain, w_t, wb_own, wz_oth, wx_oth, wb_oth, go_hand, gz_hand,
        gx.reshape(5, 2, 2, 2, 48, D), small,
    )


def contract_rows(left, right):
    left, right = left.reshape(-1, left.shape[2]), right.reshape(-1, right.shape[2])
    return lax.dot_general(
        left, right, (((0,), (0,)), ((), ())), preferred_element_type=F32
    ).astype(BF)


def body(
    hidden_in, segment_ids, norm_gain, in_weight, conv_weight, conv_bias, dt_bias, a_log, d_skip,
    gate_gain, out_weight, cotangent,
):
    shard = lax.axis_index("shard")
    tokens = hidden_in.shape[0]
    chunks = tokens // Q

    small = [norm_gain, conv_bias, dt_bias, a_log, d_skip, gate_gain, conv_weight.reshape(-1)]
    vector = jnp.concatenate(small)
    vector = jnp.pad(vector, (0, VEC * 128 - vector.shape[0])).reshape(VEC, 128)
    w_t = in_weight.T
    w_b = jnp.pad(w_t[2 * DI :], ((0, 384 - (CW - DI) - H), (0, 0)))
    wx, wb, both, normed2, g2, raw, xd = gather(hidden_in, vector, w_t, w_b, cotangent)
    wx, wb = wx.reshape(DI, -1), wb.reshape(384, -1)

    both = both.reshape(2, VEC * 128)
    whole, at = [], 0
    for value in small:
        whole.append(both[:, at : at + value.size])
        at += value.size
    gain, cbias, dtb, alog, skip, ggain = [v.reshape(-1) for v in whole[:6]]
    cweight = whole[6].reshape(2, CONV, CW // 2).transpose(1, 0, 2).reshape(CONV, CW)
    prm = jnp.concatenate(
        [
            jnp.pad(cweight, ((0, 0), (0, XD - CW))),
            jnp.pad(cbias, (0, XD - CW))[None],
            jnp.pad(jnp.repeat(skip, HEADDIM), (0, XD - DI))[None],
            jnp.pad(dtb, (0, XD - H))[None],
            jnp.pad(alog, (0, XD - H))[None],
        ]
    )
    seg = segment_ids.reshape(tokens)
    none = jnp.full((3,), -1, jnp.int32)
    before = jnp.concatenate([none, seg])
    after = jnp.concatenate([seg, none])
    by_chunk = seg.reshape(chunks, Q)
    last = by_chunk[:, -1:]
    earlier = jnp.concatenate([none[:1, None], last[:-1]])
    columns = [seg]
    columns += [before[3 - k : 3 - k + tokens] == seg for k in (1, 2, 3)]
    columns += [(by_chunk == earlier).reshape(-1), (by_chunk == last).reshape(-1)]
    columns += [after[k : k + tokens] == seg for k in (1, 2, 3)]
    columns += [jnp.zeros_like(seg)] * 7
    segc = jnp.stack([v.astype(F32) for v in columns], axis=1)
    segr = jnp.broadcast_to(by_chunk.astype(F32)[:, None, :], (chunks, 8, Q))

    ind, ind2, ind_t, rho_t = spread_consts()
    cum3, ex, cumt = prep(raw, prm, segc)
    y, sin, conv, wz, wo = scan_fwd(
        xd, segc, segr, cum3, ex, cumt, prm, ind, ind2, w_t, out_weight
    )
    wz, wo = wz.reshape(DI, -1), wo.reshape(DI // 2, D)
    gn2, dz2, dz, dy, block_out, gg = gate(
        y, normed2, cotangent, hidden_in, w_t, wz, out_weight, wo, ggain[None, :]
    )
    go = contract_rows(gn2, g2)
    gz = contract_rows(dz2, normed2)
    dxd, dx2, pg, go_hand, gz_hand, go0, gz0 = scan_bwd(
        xd, conv, dy, sin, segc, segr, cum3, ex, cumt, prm, ind, ind2, ind_t, rho_t, go, gz
    )
    gx = contract_rows(dx2, normed2)
    grads = [
        jnp.zeros((D,), F32), pg[4, :CW], pg[6, :H], pg[7, :H], pg[5, :DI].reshape(H, HEADDIM).sum(1), gg[0],
        pg[:CONV, :CW].reshape(CONV, 2, CW // 2).transpose(1, 0, 2).reshape(2, -1),
    ]
    packed = jnp.concatenate([v.reshape(2, -1) for v in grads], axis=1)
    packed = jnp.pad(packed, ((0, 0), (0, VEC * 128 - packed.shape[1]))).reshape(2, VEC, 128)
    input_grad, _, go1, gz1, gx, gb, packed = tail(
        dz, dxd, hidden_in, cotangent, gain[None, :], w_t, w_b, wz, wx, wb, go_hand, gz_hand,
        gx, packed,
    )
    own_inner, own_outer = widen(gz0, gz1, gx, gb, go0, go1)
    packed = packed.reshape(-1)
    owned, at = [], 0
    for value in small:
        owned.append(packed[at : at + value.size])
        at += value.size
    own_gain, own_cbias, own_dtb, own_alog, own_skip, own_gg, own_cw = owned
    return (
        block_out, input_grad, own_gain, own_inner.T, own_cw.reshape(conv_weight.shape), own_cbias,
        own_dtb, own_alog, own_skip, own_gg, own_outer,
    )


def solution(mesh):
    rows, half = P(("rep", "shard"), None), P("shard")
    wide, taps = P("shard", None), P(None, "shard")
    in_specs = (rows, rows, half, wide, taps, half, half, half, half, half, wide, rows)
    out_specs = (rows, rows, half, wide, taps, half, half, half, half, half, wide)
    return jax.shard_map(body, mesh=mesh, in_specs=in_specs, out_specs=out_specs, check_vma=False)
```

time: 2910 us -> 555 us (0.19)
  waiting for transfers between devices: 1050 us -> 0 us
  local copies, waits for them, and re-layouts: 921 us -> 28.1 us
  Pallas kernels: 0 us -> 465 us
  matrix products: 506 us -> 47.1 us
  other arithmetic: 260 us -> 3.28 us
  blocking collectives: 95.4 us -> 0 us
  loops' own time: 40.9 us -> 0 us
    dynamic_update_slice x40 -> x0, local copies, waits for them, and re-layouts: 616 us -> none  [scan_row(): lax.scan(jax.checkpoint(span_step), (start_state, segments[0]), (split(si...]
    pallas_call x0 -> x7, Pallas kernels: none -> 465 us  [the longest x1 133 us: tail(): pl.pallas_call(functools.partial(tail_kernel, bits), grid=(tokens // rows...]
    dot_general x60 -> x0, matrix products: 460 us -> none  [the longest x12 192 us: span_step(): jnp.einsum('hts,shp->thp', decayed * scores[None], scaled_x, precision=HIGH)]
    reduce_scatter x2 -> x0, waiting for transfers between devices: 432 us -> none  [the longest x1 432 us: body(): lax.psum_scatter(grad_inner, 'shard', scatter_dimension=0, tiled=True)]
    psum x1 -> x0, waiting for transfers between devices: 405 us -> none  [body(): lax.psum((owned[0], owned[1], owned[2], owned[3], owned[4], owned[5], own...]
    all_gather x2 -> x0, waiting for transfers between devices: 207 us -> none  [the longest x1 207 us: body(): lax.all_gather(in_weight, 'shard', axis=0, tiled=True)]
    reduce_sum x14 -> x1, other arithmetic: 97.3 us -> 0.11 us  [body(): pg[5, :DI].reshape(H, HEADDIM).sum(1)]
    mul x33 -> x0, other arithmetic: 71.8 us -> none  [the longest x1 33.1 us: mixer_row(): jax.nn.silu(conv_row(channels, segments, conv_weight, conv_bias))]
  transfers between devices with their start and end apart: 6 -> 0, of which waited for: 3 -> 0; matrix products, arithmetic and copies ran while one was open for 57% -> 0% of each run, Pallas kernels for 0% -> 0%
where the time goes in v1:
time: 555 us; the launch traced here: 545 us
  Pallas kernels  465 us (84%)
  matrix products  47.1 us (8%)
  local copies, waits for them, and re-layouts  28.1 us (5%)
    pallas_call x1, Pallas kernels, tail(): pl.pallas_call(functools.partial(tail_kernel, bits), grid=(tokens // rows...  133 us
    pallas_call x1, Pallas kernels, scan_bwd(): pl.pallas_call(functools.partial(bwd_kernel, bits), grid=(chunks,), in_sp...  127 us
    pallas_call x1, Pallas kernels, scan_fwd(): pl.pallas_call(fwd_kernel, grid=(chunks,), in_specs=[pl.BlockSpec((Q, XD)...  68.2 us
    pallas_call x1, Pallas kernels, gather(): pl.pallas_call(gather_kernel, in_specs=[vmem, vmem, hbm, hbm, hbm], out_s...  64.3 us
    pallas_call x1, Pallas kernels, gate(): pl.pallas_call(gate_kernel, grid=(tokens // rows,), in_specs=[pl.BlockSpe...  51.9 us
    dot_general x3, matrix products, contract_rows(): lax.dot_general(left, right, (((0,), (0,)), ((), ())), preferred_element_...  47.1 us
    pallas_call x1, Pallas kernels, widen(): pl.pallas_call(widen_kernel, grid=(9,), in_specs=[rows(768, half, 0, firs...  17.4 us

profile of v1, /device:TPU:0, one launch (start us, length us, event | category | flops | bytes accessed | tf_op | source)
XLA Modules:
  0.0 545.0 jit_solution(553951504768312127)
XLA Ops:
  0.6 0.8 slice.98
  1.6 0.7 convert_element_type.70
  2.3 0.8 slice.99
  3.3 0.7 compare_convert_fusion
  4.0 0.7 bitcast_convert_fusion.3
  4.6 1.0 fusion.6
  6.4 0.8 reshape.186
  7.2 0.9 concatenate.18
  8.7 1.0 copy.54.segc_ref
  9.7 1.1 slice.125
  10.7 0.9 pad.34.wb_ref.wb_own
  11.6 64.3 %gather.1 = (bf16[2,2,2,384,768]{4,3,2,1,0:T(8,128)(2,1)}, bf16[2,2,2,48,768]{4,3,2,1,0:T(8,128)(2,1)}, f32[2,88,128]{2,1,0:T(8,128)}, bf16[2,1024,1536]{2,1,0:T...) custom-call(bf16[1024,1536]{1,0:T(8,128)(2,1)} %u_ref.5, ...), custom_call_target="tpu_custom_call" | custom-call | flops 11000000512 | bytes 40000000 | tf_op jit(solution)/shard_map/gather/pallas_call | solution.py:1210
  75.9 0.9 copy.72
  78.9 0.7 concatenate.22.prm_ref
  79.6 3.7 prep.1
  83.3 68.2 %scan_fwd.1 = (f32[1024,3072]{1,0:T(8,128)}, bf16[8,128,3072]{2,1,0:T(8,128)(2,1)}, f32[1024,3328]{1,0:T(8,128)}, bf16[2,2,2,384,768]{4,3,2,1,0:T(8,128)(2,1)}, bf16[2,2,2,192,1536]{4,3,2,1,0:T(8,128)(2,1)}) custom-call(f32[1024,3456]{1,0:T(8,128)} %get-tuple-element.47.xd_ref, f32[1024,16]{1,0:T(8,128)} %copy.54.segc_ref, ...), custom_call_target="tpu_custom_call" | custom-call | flops 20000000000 | bytes 38000000 | tf_op jit(solution)/shard_map/scan_fwd/pallas_call | solution.py:550
  151.5 51.9 %gate.1 = (bf16[2,1024,1536]{2,1,0:T(8,128)(2,1)}, bf16[2,1024,1536]{2,1,0:T(8,128)(2,1)}, bf16[1024,3072]{1,0:T(8,128)(2,1)}, bf16[1024,3072]{1,0:T(8,128)(2,1)...) custom-call(f32[1024,3072]{1,0:T(8,128)} %get-tuple-element.53.y_ref, bf16[2,1024,1536]{2,1,0:T(8,128)(2,1)} %get-tuple-element.54.nrm_ref, ...), custom_call_target="tpu_custom_call" | custom-call | flops 28999999488 | bytes 64000000 | tf_op jit(solution)/shard_map/gate/pallas_call | solution.py:700
  203.4 15.8 %bitcast_convert_fusion.2 = bf16[1536,1536]{1,0:T(8,128)(2,1)} fusion(bf16[2,1024,1536]{2,1,0:T(8,128)(2,1)} %get-tuple-element.62, bf16[2,1024,1536]{2,1,0:T(8,128)(2,1)} %get-tuple-element.63), kind=kOutput, calls=%fused_computation.2 | convolution fusion | flops 9666035712 | bytes 17301504 | tf_op jit(solution)/shard_map/dot_general | solution.py:1493
  219.2 13.6 %bitcast_convert_fusion.1 = bf16[1536,1536]{1,0:T(8,128)(2,1)} fusion(bf16[2,1024,1536]{2,1,0:T(8,128)(2,1)S(1)} %copy-done.2, bf16[2,1024,1536]{2,1,0:T(8,128)(2,1)} %get-tuple-element.54.nrm_ref), kind=kOutput, calls=%fused_computation.1 | convolution fusion | flops 9666035712 | bytes 17301504 | tf_op jit(solution)/shard_map/dot_general | solution.py:1493
  232.8 127.1 %scan_bwd.1 = (bf16[1024,3456]{1,0:T(8,128)(2,1)}, bf16[2,1024,1920]{2,1,0:T(8,128)(2,1)}, f32[8,3456]{1,0:T(8,128)}, bf16[2,32,1536]{2,1,0:T(8,128)(2,1)}, bf16...) custom-call(f32[1024,3456]{1,0:T(8,128)} %get-tuple-element.47.xd_re, ...), custom_call_target="tpu_custom_call" | custom-call | flops 60000002048 | bytes 50000000 | tf_op jit(solution)/shard_map/scan_bwd/pallas_call | solution.py:1002
  359.8 1.0 slice_reduce_fusion.1
  360.9 17.8 %bitcast_convert_fusion = bf16[1920,1536]{1,0:T(8,128)(2,1)} fusion(bf16[2,1024,1920]{2,1,0:T(8,128)(2,1)} %get-tuple-element.70, bf16[2,1024,1536]{2,1,0:T(8,128)(2,1)} %get-tuple-element.54.nrm_ref), kind=kOutput, calls=%fused_computation | convolution fusion | flops 12082544640 | bytes 20054016 | tf_op jit(solution)/shard_map/dot_general | solution.py:1493
  379.5 0.6 copy.71
  380.1 132.8 %tail.1 = (f32[1024,1536]{1,0:T(8,128)}, f32[8,1536]{1,0:T(8,128)}, bf16[2,2,2,2,2,32,1536]{6,5,4,3,2,1,0:T(8,128)(2,1)}, bf16[2,2,2,2,2,48,768]{6,5,4,3,2,1,0:T...) custom-call(bf16[1024,3072]{1,0:T(8,128)(2,1)} %get-tuple-element.58, ...), custom_call_target="tpu_custom_call" | custom-call | flops 20500000768 | bytes 80000000 | tf_op jit(solution)/shard_map/tail/pallas_call | solution.py:1449
  513.0 1.4 fusion.13
  514.3 1.3 slice_bitcast_fusion.3
  515.6 1.4 slice.137
  517.0 1.3 slice_bitcast_fusion.1
  518.3 0.8 slice.133
  519.8 17.4 %widen.1 = (f32[6448,768]{1,0:T(8,128)}, f32[1536,1536]{1,0:T(8,128)}) custom-call(bf16[1536,768]{1,0:T(8,128)(2,1)} %bitcast.78, bf16[1536,768]{1,0:T(8,128)(2,1)} %bitcast.79, bf16[3072,768]{1,0:T(8,128)(2,1)} %bitcast.76, bf16[384,768]{1,0:T(8,128)(2,1)} %bitcast.81, bf16[512,1536]{1,0:T(8,128)(2,1)} %bitcast.80, bf16[1024,1536]{1,0:T(8,128)(2,1)} %bitcast.77), custom_call_target="tpu_custom_call" | custom-call | bytes 44000000 | tf_op jit(solution)/shard_map/widen/pallas_call | solution.py:780
  537.2 1.7 copy.75
  538.9 5.9 %copy.76 = f32[1024,1536]{1,0:T(8,128)} copy(f32[1024,1536]{1,0:T(8,128)} %get-tuple-element.113) | data formatting | bytes 12582912
  (55 shorter events, 5.2 us)
Async XLA Ops:
  203.4 15.8 %copy-start.2 = (bf16[2,1024,1536]{2,1,0:T(8,128)(2,1)S(1)}, bf16[2,1024,1536]{2,1,0:T(8,128)(2,1)}, u32[]{:S(2)}) copy-start(bf16[2,1024,1536]{2,1,0:T(8,128)(2,1)} %get-tuple-element.64) | copy-start | bytes 18874372
  360.9 17.8 %copy-start.1 = (f32[8,3456]{1,0:T(8,128)S(1)}, f32[8,3456]{1,0:T(8,128)}, u32[]{:S(2)}) copy-start(f32[8,3456]{1,0:T(8,128)} %get-tuple-element.71) | copy-start | bytes 331780
  519.8 17.4 %copy-start = (bf16[1024,1536]{1,0:T(8,128)(2,1)S(1)}, bf16[1024,1536]{1,0:T(8,128)(2,1)}, u32[]{:S(2)}) copy-start(bf16[1024,1536]{1,0:T(8,128)(2,1)} %get-tuple-element.112) | copy-start | bytes 9437188
